TPU v7x, 32 devices: a whole 2x2x4 slice. The times are simulated.
32 devices in a mesh: req: 8 (over z, x), mlp: 4 (over y, core).
Axes of the slice: x: 2, y: 2, z: 4, core: 2. Of those that a mesh axis runs over, the one named last changes fastest.
Arguments:
- patches: bfloat16 [7680, 4096], P('req'), may hold values from -6 to 6
- norm_gain: float32 [4096], replicated, may hold values from 0.25 to 1.75
- norm_bias: float32 [4096], replicated, may hold values from -3 to 3
- gate_weight: bfloat16 [4096, 8192], P(None, ('req', 'mlp')), may hold values from -0.09375 to 0.09375
- up_weight: bfloat16 [4096, 8192], P(None, ('req', 'mlp')), may hold values from -0.09375 to 0.09375
- down_weight: bfloat16 [4096, 8192], P(None, ('req', 'mlp')), may hold values from -0.0625 to 0.0625
- layer_scale: float32 [4096], replicated, may hold values from 0.25 to 2.5
- projection: bfloat16 [4, 4096, 4096], P(None, 'mlp', 'req'), may hold values from -0.046875 to 0.046875
- text_rows: bfloat16 [32768, 4096], P(('req', 'mlp')), may hold values from -6 to 6
- destination: int32 [1920], replicated, may hold values from -1 to 32767, as said below
Outputs:
- patch_out: bfloat16 [7680, 4096], P('req', 'mlp')
- streams: bfloat16 [32768, 4096], P(('req', 'mlp'))
Inputs may be any that keep to these rules, and one draw needn't show every extreme that they name: `destination`: values other than -1 are distinct positions; the positions landing in one piece of 1024 consecutive positions (a stream holds 4 pieces) form one run of consecutive positions, at least one and at most 60 of them, and some piece receives exactly 60.
All inputs are finite; a program needn't handle non-finite values.
Results may differ from a plain program's by a relative error of at most 0.015.
Values may be sent and summed in bfloat16 or wider, within the bound.
A program may use at most 128 MiB of HBM per device.

v0:
```python
import jax
import jax.numpy as jnp
from jax import lax
from jax.sharding import PartitionSpec as P


def layer_norm(values, norm_gain, norm_bias):
    row_mean = jnp.mean(values, axis=-1, keepdims=True)
    centred = values - row_mean
    variance = jnp.mean(centred * centred, axis=-1, keepdims=True)
    return centred * lax.rsqrt(variance + 1e-06) * norm_gain + norm_bias


def shards(
    patches,
    norm_gain,
    norm_bias,
    gate_weight,
    up_weight,
    down_weight,
    layer_scale,
    projection,
    text_rows,
    destination,
):
    req_count = lax.axis_size("req")
    mlp_count = lax.axis_size("mlp")
    req_index = lax.axis_index("req")
    mlp_index = lax.axis_index("mlp")
    rows_here, model_width = patches.shape
    feat_width = model_width // mlp_count
    inputs = patches.astype(jnp.float32)
    normed = layer_norm(inputs, norm_gain, norm_bias).astype(jnp.bfloat16)
    gate_act = jnp.dot(
        normed,
        lax.all_gather(gate_weight, "req", axis=1, tiled=True),
        preferred_element_type=jnp.float32,
    )
    up_act = jnp.dot(
        normed,
        lax.all_gather(up_weight, "req", axis=1, tiled=True),
        preferred_element_type=jnp.float32,
    )
    hidden = (jax.nn.silu(gate_act) * up_act).astype(jnp.bfloat16)
    ffn_local = lax.dot_general(
        hidden,
        lax.all_gather(down_weight, "req", axis=1, tiled=True),
        (((1,), (1,)), ((), ())),
        preferred_element_type=jnp.float32,
    )
    partial_value = lax.optimization_barrier(ffn_local.astype(jnp.bfloat16)).astype(jnp.float32)
    ffn_feats = lax.psum_scatter(
        partial_value.astype(jnp.bfloat16), "mlp", scatter_dimension=1, tiled=True
    ).astype(jnp.float32)
    scale_here = lax.dynamic_slice_in_dim(layer_scale, mlp_index * feat_width, feat_width)
    own_inputs = lax.dynamic_slice_in_dim(inputs, mlp_index * feat_width, feat_width, axis=1)
    patch_out = (own_inputs + scale_here * ffn_feats).astype(jnp.bfloat16)
    merged = patch_out.reshape(rows_here // 4, 4 * feat_width)
    weight_cols = projection.reshape(4 * feat_width, projection.shape[2])
    piece_rows = text_rows.shape[0]
    slot_count = destination.shape[0]
    bucket_count = req_count * mlp_count
    capacity = slot_count // bucket_count
    is_valid = destination >= 0
    piece_ids = jnp.where(is_valid, destination // piece_rows, -1)
    offsets = destination % piece_rows
    bucket_hit = piece_ids[:, None] == jnp.arange(bucket_count, dtype=jnp.int32)[None, :]
    first_off = jnp.min(jnp.where(bucket_hit, offsets[:, None], piece_rows), axis=0)
    counts = jnp.sum(bucket_hit.astype(jnp.int32), axis=0)
    slot_first = jnp.sum(jnp.where(bucket_hit, first_off[None, :], 0), axis=1)
    slot_rank = offsets - slot_first
    stream_ids = piece_ids // mlp_count
    piece_in = piece_ids % mlp_count
    rows_at = piece_in * (req_count * capacity) + stream_ids * capacity + slot_rank
    rows_at = jnp.where(is_valid, rows_at, bucket_count * capacity)
    sources = (
        jnp.full((bucket_count * capacity,), -1, jnp.int32)
        .at[rows_at]
        .set(jnp.arange(slot_count, dtype=jnp.int32), mode="drop")
    )
    every_row = lax.all_gather(merged, "req", axis=0, tiled=True)
    picked_rows = jnp.take(every_row, jnp.maximum(sources, 0), axis=0)
    picked_rows = jnp.where(sources[:, None] >= 0, picked_rows, jnp.zeros_like(picked_rows))
    summed = lax.psum_scatter(
        jnp.dot(picked_rows, weight_cols, preferred_element_type=jnp.float32).astype(jnp.bfloat16),
        "mlp",
        scatter_dimension=0,
        tiled=True,
    )
    arrived = lax.all_to_all(summed, "req", split_axis=0, concat_axis=1, tiled=True)
    bucket_here = req_index * mlp_count + mlp_index
    start_here = first_off[bucket_here]
    count_here = counts[bucket_here]
    positions = jnp.arange(piece_rows, dtype=jnp.int32) - start_here
    inside = (positions >= 0) & (positions < count_here)
    image_rows = jnp.take(arrived, jnp.clip(positions, 0, capacity - 1), axis=0)
    streams = jnp.where(inside[:, None], image_rows, text_rows)
    return (patch_out, streams)


def solution(mesh):
    return jax.shard_map(
        shards,
        mesh=mesh,
        in_specs=(
            P("req", None),
            P(),
            P(),
            P(None, ("req", "mlp")),
            P(None, ("req", "mlp")),
            P(None, ("req", "mlp")),
            P(),
            P(None, "mlp", "req"),
            P(("req", "mlp"), None),
            P(),
        ),
        out_specs=(P("req", "mlp"), P(("req", "mlp"), None)),
        check_vma=False,
    )
```

profile of v0, /device:TPU:0, one launch (start us, length us, event | category | flops | bytes accessed | tf_op | source)
XLA Modules:
  0.0 1134.5 jit_solution(1974521009952528211)
XLA Ops:
  9.5 4.5 convert_reduce_fusion
  13.9 1.0 copy-done
  14.9 2.2 multiply_reduce_fusion
  17.1 223.4 %all-gather.5.cloned.1.call-done = bf16[4096,2048]{1,0:T(8,128)(2,1)} async-done(((bf16[4096,256]{1,0:T(8,128)(2,1)}), bf16[4096,2048]{1,0:T(8,128)(2,1)}) %all-gather.5.cloned.1.call-update) | async-done | bytes 16777232 | tf_op jit(solution)/shard_map/all_gather | solution.py:36
  240.5 23.2 %fusion.32 = f32[960,2048]{1,0:T(8,128)} fusion(bf16[4096,2048]{1,0:T(8,128)(2,1)} %all-gather.5.cloned.1.call-done, bf16[960,4096]{1,0:T(8,128)(2,1)} %param.10, f32[4096]{0:T(1024)S(1)} %copy-done.3, f32[4096]{0:T(1024)S(1)} %copy-done.4, f32[960]{0:T(1024)S(1)} %add_rsqrt_fusion, f32[960]{0:T(1024)S(1)} %broadcast_multiply_fusion), kind=kOutput, calls=%fused_computation.68 | convolution fusion | flops 16129720320 | bytes 32546304 | tf_op jit(solution)/shard_map/dot_general | solution.py:34
  263.7 204.8 %all-gather.7.cloned.1.call-done = bf16[4096,2048]{1,0:T(8,128)(2,1)} async-done(((bf16[4096,256]{1,0:T(8,128)(2,1)}), bf16[4096,2048]{1,0:T(8,128)(2,1)}) %all-gather.7.cloned.1.call-update) | async-done | bytes 16777232 | tf_op jit(solution)/shard_map/all_gather | solution.py:41
  468.5 25.3 %multiply_convert_fusion = bf16[960,2048]{1,0:T(8,128)(2,1)} fusion(f32[960,2048]{1,0:T(8,128)} %fusion.32, bf16[4096,2048]{1,0:T(8,128)(2,1)} %all-gather.7.cloned.1.call-done, bf16[960,4096]{1,0:T(8,128)(2,1)} %param.10, f32[4096]{0:T(1024)S(1)} %copy-done.3, f32[4096]{0:T(1024)S(1)} %copy-done.4, f32[960]{0:T(1024)S(1)} %add_rsqrt_fusion, ...), kind=kOutput, calls=%fused_computation.14 | convolution fusion | flops 16141516800 | bytes 36478464 | tf_op jit(solution)/shard_map/dot_general | solution.py:39
  493.8 202.7 %all-gather.9.cloned.1.call-done = bf16[4096,2048]{1,0:T(8,128)(2,1)} async-done(((bf16[4096,256]{1,0:T(8,128)(2,1)}), bf16[4096,2048]{1,0:T(8,128)(2,1)}) %all-gather.9.cloned.1.call-update) | async-done | bytes 16777232 | tf_op jit(solution)/shard_map/all_gather | solution.py:47
  696.6 23.3 %convolution_convert_fusion = bf16[960,4096]{1,0:T(8,128)(2,1)} fusion(bf16[960,2048]{1,0:T(8,128)(2,1)} %multiply_convert_fusion, bf16[4096,2048]{1,0:T(8,128)(2,1)} %all-gather.9.cloned.1.call-done), kind=kOutput, calls=%fused_computation.15 | convolution fusion | flops 16110059520 | bytes 28573696 | tf_op jit(solution)/shard_map/dot_general | solution.py:45
  719.9 13.1 %convert_element_type.26 = f32[960,4096]{1,0:T(8,128)} convert(bf16[960,4096]{1,0:T(8,128)(2,1)} %param.10) | non-fusion elementwise | flops 3932160 | bytes 23592960 | tf_op jit(solution)/shard_map/convert_element_type | solution.py:32
  733.7 53.5 %reduce-scatter.3.cloned.1.call-done = bf16[960,1024]{1,0:T(8,128)(2,1)} async-done(((bf16[960,4096]{1,0:T(8,128)(2,1)}), bf16[960,1024]{1,0:T(8,128)(2,1)}) %reduce-scatter.3.cloned.1.call-update) | async-done | bytes 1966096 | tf_op jit(solution)/shard_map/reduce_scatter | solution.py:52
  787.2 3.4 add_convert_fusion.1
  790.6 2.7 reshape.67
  793.8 10.2 scatter_custom_fusion
  804.0 204.3 %all-gather.11.cloned.1.call-done = bf16[1920,4096]{1,0:T(8,128)(2,1)} async-done(((bf16[240,4096]{1,0:T(8,128)(2,1)}), bf16[1920,4096]{1,0:T(8,128)(2,1)}) %all-gather.11.cloned.1.call-update) | async-done | bytes 15728656 | tf_op jit(solution)/shard_map/all_gather | solution.py:81
  1008.3 36.0 %gather_fusion = bf16[1920,4096]{1,0:T(8,128)(2,1)} fusion(bf16[1920,4096]{1,0:T(8,128)(2,1)} %all-gather.11.cloned.1.call-done, s32[2048]{0:T(1024)S(1)} %pad_clamp_fusion), kind=kCustom, calls=%fused_computation | custom fusion | bytes 31464960 | tf_op jit(solution)/shard_map/jit(_take)/gather | solution.py:82
  1044.3 14.4 %fusion.7 = bf16[1920,512]{1,0:T(8,128)(2,1)} fusion(bf16[4096,512]{1,0:T(8,128)(2,1)} %bitcast.17, bf16[1920,4096]{1,0:T(8,128)(2,1)} %gather_fusion, pred[1920]{0:T(1024)(128)(4,1)S(1)} %get-tuple-element.5, pred[1920]{0:T(1024)(128)(4,1)S(1)} %get-tuple-element.4), kind=kOutput, calls=%fused_computation.17 | convolution fusion | flops 8069775360 | bytes 21892864 | tf_op jit(solution)/shard_map/dot_general | solution.py:85
  1058.7 29.0 %reduce-scatter.5.cloned.1.call-done = bf16[480,512]{1,0:T(8,128)(2,1)} async-done(((bf16[1920,512]{1,0:T(8,128)(2,1)}), bf16[480,512]{1,0:T(8,128)(2,1)}) %reduce-scatter.5.cloned.1.call-update) | async-done | bytes 491536 | tf_op jit(solution)/shard_map/reduce_scatter | solution.py:84
  1087.7 1.9 all_to_all.14
  1089.6 5.5 all-to-all-start
  1096.4 1.3 fusion.28
  1098.3 11.3 all-to-all-done
  1110.1 7.6 gather_fusion.1
  1117.7 9.5 select_select_fusion
  (39 shorter events, 5.9 us)
Async XLA Ops:
  7.2 233.4 %all-gather.5.cloned.1.call-start = ((), (), s32[]{:S(2)}) async-start(), calls=%async_computation.3 | async-start | bytes 18874368 | tf_op jit(solution)/shard_map/all_gather | solution.py:36
  7.9 460.6 %all-gather.7.cloned.1.call-start = ((), (), s32[]{:S(2)}) async-start(), calls=%async_computation.4 | async-start | bytes 18874368 | tf_op jit(solution)/shard_map/all_gather | solution.py:41
  8.6 687.9 %all-gather.9.cloned.1.call-start = ((), (), s32[]{:S(2)}) async-start(), calls=%async_computation.5 | async-start | bytes 18874368 | tf_op jit(solution)/shard_map/all_gather | solution.py:47
  9.4 777.8 %reduce-scatter.3.cloned.1.call-start = ((), (), s32[]{:S(2)}) async-start(), calls=%async_computation.6 | async-start | bytes 9830400 | tf_op jit(solution)/shard_map/reduce_scatter | solution.py:52
  9.4 5.5 copy-start
  9.4 231.1 %copy-start.3 = (f32[4096]{0:T(1024)S(1)}, f32[4096]{0:T(1024)}, u32[]{:S(2)}) copy-start(f32[4096]{0:T(1024)} %param.12) | copy-start | bytes 49156
  9.5 231.1 %copy-start.4 = (f32[4096]{0:T(1024)S(1)}, f32[4096]{0:T(1024)}, u32[]{:S(2)}) copy-start(f32[4096]{0:T(1024)} %param.11) | copy-start | bytes 49156
  719.8 288.5 %all-gather.11.cloned.1.call-start = ((), (), s32[]{:S(2)}) async-start(), calls=%async_computation.7 | async-start | bytes 17694720 | tf_op jit(solution)/shard_map/all_gather | solution.py:81
  732.9 60.5 %copy-start.2 = (s32[1920]{0:T(1024)S(1)}, s32[1920]{0:T(1024)}, u32[]{:S(2)}) copy-start(s32[1920]{0:T(1024)} %param.19) | copy-start | bytes 23044
  790.6 253.7 %copy-start.1 = (bf16[960,1024]{1,0:T(8,128)(2,1)}, bf16[960,1024]{1,0:T(8,128)(2,1)S(1)}, u32[]{:S(2)}) copy-start(bf16[960,1024]{1,0:T(8,128)(2,1)S(1)} %add_convert_fusion.1) | copy-start | bytes 5898244
  793.4 294.4 %reduce-scatter.5.cloned.1.call-start = ((), (), s32[]{:S(2)}) async-start(), calls=%async_computation.8 | async-start | bytes 2457600 | tf_op jit(solution)/shard_map/reduce_scatter | solution.py:84
  1089.6 20.0 %all-to-all-start = ((bf16[8,60,512]{2,1,0:T(8,128)(2,1)}), bf16[8,60,512]{2,1,0:T(8,128)(2,1)S(1)}, u32[]{:S(2)}, u32[]{:S(2)}) async-start(bf16[8,60,512]{2,1,0:T(8,128)(2,1)} %all_to_all.14), calls=%async_computation.2 | async-start | bytes 1048576 | tf_op jit(solution)/shard_map/all_to_all | solution.py:90
Sparse Core Ops, SparseCore 0:
  10.0 230.4 all-gather.4
  242.6 225.9 all-gather.6
  470.6 225.9 all-gather.8
  720.0 67.1 reduce-scatter.2
  793.5 214.7 all-gather.10
  1058.8 28.8 reduce-scatter.4
where the time goes:
time: 1140 us; the launch traced here: 1130 us
  waiting for transfers between devices  931 us (82%)
  matrix products  86.1 us (8%)
  local copies, waits for them, and re-layouts  61.8 us (5%)
  other arithmetic  34.9 us (3%)
  between operations  14.7 us (1%)
    all_gather x1, waiting for transfers between devices, shards(): lax.all_gather(gate_weight, 'req', axis=1, tiled=True)  223 us
    all_gather x1, waiting for transfers between devices, shards(): lax.all_gather(up_weight, 'req', axis=1, tiled=True)  205 us
    all_gather x1, waiting for transfers between devices, shards(): every_row = lax.all_gather(merged, 'req', axis=0, tiled=True)  204 us
    all_gather x1, waiting for transfers between devices, shards(): lax.all_gather(down_weight, 'req', axis=1, tiled=True)  203 us
    reduce_scatter x1, waiting for transfers between devices, shards(): lax.psum_scatter(partial_value.astype(jnp.bfloat16), 'mlp', scatter_dimen...  53.5 us
    gather x1, local copies, waits for them, and re-layouts, shards(): picked_rows = jnp.take(every_row, jnp.maximum(sources, 0), axis=0)  36 us
    reduce_scatter x1, waiting for transfers between devices, shards(): lax.psum_scatter(jnp.dot(picked_rows, weight_cols, preferred_element_type...  29 us
    dot_general x1, matrix products, shards(): jnp.dot(normed, lax.all_gather(up_weight, 'req', axis=1, tiled=True), pre...  25.3 us
  transfers between devices with their start and end apart: 7, of which 7 were waited for; matrix products, arithmetic and copies ran while one was open for 7% of the time, Pallas kernels for 0%

commit v1 on v0

v1 whole, which is shorter than its diff:
```python
import jax
import jax.numpy as jnp
from jax import lax
from jax.sharding import PartitionSpec as P


def layer_norm(values, norm_gain, norm_bias):
    row_mean = jnp.mean(values, axis=-1, keepdims=True)
    centred = values - row_mean
    variance = jnp.mean(centred * centred, axis=-1, keepdims=True)
    return centred * lax.rsqrt(variance + 1e-06) * norm_gain + norm_bias


def shards(
    patches,
    norm_gain,
    norm_bias,
    gate_weight,
    up_weight,
    down_weight,
    layer_scale,
    projection,
    text_rows,
    destination,
):
    req_count = lax.axis_size("req")
    mlp_count = lax.axis_size("mlp")
    req_index = lax.axis_index("req")
    mlp_index = lax.axis_index("mlp")
    far_count = 4
    near_count = req_count // far_count
    pair_count = mlp_count // 2
    far, near = req_index // near_count, req_index % near_count
    pair, core = mlp_index // 2, mlp_index % 2

    def shift_far(x, s):
        perm = [
            (f * near_count + n, ((f + s) % far_count) * near_count + n)
            for f in range(far_count)
            for n in range(near_count)
        ]
        return lax.ppermute(x, "req", perm)

    def shift_near(x, s):
        perm = [
            (f * near_count + n, f * near_count + (n + s) % near_count)
            for f in range(far_count)
            for n in range(near_count)
        ]
        return lax.ppermute(x, "req", perm)

    def shift_pair(x, s):
        perm = [(p * 2 + c, ((p + s) % pair_count) * 2 + c) for p in range(pair_count) for c in range(2)]
        return lax.ppermute(x, "mlp", perm)

    def swap_core(x):
        return lax.ppermute(x, "mlp", [(m, m ^ 1) for m in range(mlp_count)])

    rows_here, model_width = patches.shape
    feat_width = model_width // mlp_count

    def with_near(w):
        return jnp.concatenate([w] + [shift_near(w, s) for s in range(1, near_count)], axis=1)

    def quarter_at(t, d, sign):
        other = (pair + sign * t) % pair_count
        return (other * 2 + (core + d) % 2) * feat_width

    def relative(x, axis, sign, which):
        return jnp.concatenate(
            [lax.dynamic_slice_in_dim(x, quarter_at(t, d, sign), feat_width, axis=axis) for t, d in which], axis=axis
        )

    both = [(t, d) for d in range(2) for t in range(pair_count)]
    kept = [(t, 0) for t in range(pair_count)]
    sent = [(t, 1) for t in range(pair_count)]

    inputs = patches.astype(jnp.float32)
    normed = layer_norm(inputs, norm_gain, norm_bias).astype(jnp.bfloat16)
    own_quarter = lax.dynamic_slice_in_dim(normed, mlp_index * feat_width, feat_width, axis=1)
    gate_full = with_near(gate_weight)
    up_full = with_near(up_weight)
    down_full = with_near(down_weight)
    gate_rel = relative(gate_full, 0, -1, both)
    up_rel = relative(up_full, 0, -1, both)
    down_sent = relative(down_full, 0, 1, sent)
    down_kept = relative(down_full, 0, 1, kept)

    def normed_block(s):
        if s == 0:
            return relative(normed, 1, -1, both)
        first = shift_far(own_quarter, s)
        column = [first] + [shift_pair(first, t) for t in range(1, pair_count)]
        return jnp.concatenate(column + [swap_core(c) for c in column], axis=1)

    blocks = [normed_block(s) for s in range(far_count)]

    def dot_t(a, w):
        return lax.dot_general(a, w, (((1,), (1,)), ((), ())), preferred_element_type=jnp.float32)

    total = None
    for s in (1, 3, 2, 0):
        block = blocks[s]
        gate_act = jnp.dot(block, gate_rel, preferred_element_type=jnp.float32)
        up_act = jnp.dot(block, up_rel, preferred_element_type=jnp.float32)
        hidden = (jax.nn.silu(gate_act) * up_act).astype(jnp.bfloat16)
        from_core = swap_core(dot_t(hidden, down_sent).astype(jnp.bfloat16))
        of_core = dot_t(hidden, down_kept) + from_core.astype(jnp.float32)
        mine = of_core[:, :feat_width]
        for t in range(1, pair_count):
            part = of_core[:, t * feat_width : (t + 1) * feat_width].astype(jnp.bfloat16)
            mine = mine + shift_pair(part, t).astype(jnp.float32)
        if s:
            mine = shift_far(mine.astype(jnp.bfloat16), far_count - s).astype(jnp.float32)
        total = mine if total is None else total + mine

    scale_here = lax.dynamic_slice_in_dim(layer_scale, mlp_index * feat_width, feat_width)
    own_inputs = lax.dynamic_slice_in_dim(patches, mlp_index * feat_width, feat_width, axis=1).astype(jnp.float32)
    patch_out = (own_inputs + scale_here * total).astype(jnp.bfloat16)

    merged = patch_out.reshape(rows_here // 4, 4 * feat_width)
    weight_cols = projection.reshape(4 * feat_width, projection.shape[2])
    slots_here = rows_here // 4
    piece_rows = text_rows.shape[0]
    slot_count = destination.shape[0]
    bucket_count = req_count * mlp_count
    capacity = slot_count // bucket_count
    is_valid = destination >= 0
    piece_ids = jnp.where(is_valid, destination // piece_rows, -1)
    offsets = destination % piece_rows
    bucket_hit = piece_ids[:, None] == jnp.arange(bucket_count, dtype=jnp.int32)[None, :]
    first_off = jnp.min(jnp.where(bucket_hit, offsets[:, None], piece_rows), axis=0)
    counts = jnp.sum(bucket_hit.astype(jnp.int32), axis=0)
    slot_first = jnp.sum(jnp.where(bucket_hit, first_off[None, :], 0), axis=1)
    rows_at = piece_ids * capacity + offsets - slot_first
    rows_at = jnp.where(is_valid, rows_at, bucket_count * capacity)
    slot_ids = jnp.arange(slot_count, dtype=jnp.int32)
    slot_req = slot_ids // slots_here
    slot_far = (far - slot_req // near_count) % far_count
    slot_near = (near - slot_req % near_count) % near_count
    slot_place = (slot_far * near_count + slot_near) * slots_here + slot_ids % slots_here
    sources = (
        jnp.zeros((bucket_count * capacity,), jnp.int32).at[rows_at].set(slot_place, mode="drop")
    )

    gathered = []
    for s in range(far_count):
        first = merged if s == 0 else shift_far(merged, s)
        gathered += [first] + [shift_near(first, t) for t in range(1, near_count)]
    products = jnp.concatenate(
        [jnp.dot(g, weight_cols, preferred_element_type=jnp.float32).astype(jnp.bfloat16) for g in gathered], axis=0
    )
    picked = jnp.take(products, sources, axis=0)
    out_width = picked.shape[1]
    arrived = lax.all_to_all(
        picked.reshape(bucket_count, capacity, out_width), ("req", "mlp"), split_axis=0, concat_axis=0, tiled=True
    )
    arrived = arrived.reshape(req_count, mlp_count, capacity, out_width).astype(jnp.float32).sum(axis=1)
    arrived = arrived.astype(jnp.bfloat16).transpose(1, 0, 2).reshape(capacity, req_count * out_width)

    bucket_here = req_index * mlp_count + mlp_index
    start_here = first_off[bucket_here]
    count_here = counts[bucket_here]
    window = jnp.minimum(start_here, piece_rows - capacity)
    ranks = jnp.arange(capacity, dtype=jnp.int32) + window - start_here
    inside = (ranks >= 0) & (ranks < count_here)
    image_rows = jnp.take(arrived, jnp.clip(ranks, 0, capacity - 1), axis=0)
    old_rows = lax.dynamic_slice_in_dim(text_rows, window, capacity, axis=0)
    new_rows = jnp.where(inside[:, None], image_rows, old_rows)
    streams = lax.dynamic_update_slice_in_dim(text_rows, new_rows, window, axis=0)
    return (patch_out, streams)


def solution(mesh):
    return jax.shard_map(
        shards,
        mesh=mesh,
        in_specs=(
            P("req", None),
            P(),
            P(),
            P(None, ("req", "mlp")),
            P(None, ("req", "mlp")),
            P(None, ("req", "mlp")),
            P(),
            P(None, "mlp", "req"),
            P(("req", "mlp"), None),
            P(),
        ),
        out_specs=(P("req", "mlp"), P(("req", "mlp"), None)),
        check_vma=False,
    )
```

time: 1140 us -> 952 us (0.84)
  waiting for transfers between devices: 931 us -> 624 us
  starting transfers between devices: 5.73 us -> 74.4 us
  local copies, waits for them, and re-layouts: 61.8 us -> 92.9 us
  matrix products: 86.1 us -> 117 us
  between operations: 14.7 us -> 2.41 us
    all_gather x4 -> x0, waiting for transfers between devices: 835 us -> none  [the longest x1 223 us: shards(): lax.all_gather(gate_weight, 'req', axis=1, tiled=True)]
    ppermute x0 -> x33, waiting for transfers between devices: none -> 579 us  [the longest x9 311 us: shift_far(): return lax.ppermute(x, 'req', perm)]
    reduce_scatter x2 -> x0, waiting for transfers between devices: 82.5 us -> none  [the longest x1 53.5 us: shards(): lax.psum_scatter(partial_value.astype(jnp.bfloat16), 'mlp', scatter_dimen...]
    unnamed x12 -> x81, local copies, waits for them, and re-layouts: 1.19 us -> 41.1 us
    all_to_all x1, starting transfers between devices: 5.5 us -> 43.9 us  [shards(): lax.all_to_all(picked.reshape(bucket_count, capacity, out_width), ('req',...]
    all_to_all x1, waiting for transfers between devices: 11.3 us -> 45.1 us  [shards(): lax.all_to_all(picked.reshape(bucket_count, capacity, out_width), ('req',...]
    gather x2 -> x3, local copies, waits for them, and re-layouts: 43.6 us -> 10.1 us  [the longest x2 9.24 us: shards(): picked = jnp.take(products, sources, axis=0)]
    dot_general x4 -> x24, matrix products: 86.1 us -> 117 us  [the longest x8 35.2 us: dot_t(): lax.dot_general(a, w, (((1,), (1,)), ((), ())), preferred_element_type=jn...]
  transfers between devices with their start and end apart: 7 -> 34, of which waited for: 7 -> 15; matrix products, arithmetic and copies ran while one was open for 7% -> 20% of each run, Pallas kernels for 0% -> 0%
where the time goes in v1:
time: 952 us; the launch traced here: 943 us
  waiting for transfers between devices  624 us (66%)
  matrix products  117 us (12%)
  local copies, waits for them, and re-layouts  92.9 us (10%)
  starting transfers between devices  74.4 us (8%)
  other arithmetic  32.9 us (3%)
    ppermute x9, waiting for transfers between devices, shift_far(): return lax.ppermute(x, 'req', perm)  311 us
    ppermute x7, waiting for transfers between devices, shift_pair(): return lax.ppermute(x, 'mlp', perm)  203 us
    ppermute x7, waiting for transfers between devices, shift_near(): return lax.ppermute(x, 'req', perm)  64.2 us
    all_to_all x1, waiting for transfers between devices, shards(): lax.all_to_all(picked.reshape(bucket_count, capacity, out_width), ('req',...  45.1 us
    all_to_all x1, starting transfers between devices, shards(): lax.all_to_all(picked.reshape(bucket_count, capacity, out_width), ('req',...  43.9 us
    unnamed x81, local copies, waits for them, and re-layouts  41.1 us
    dot_general x8, matrix products, dot_t(): lax.dot_general(a, w, (((1,), (1,)), ((), ())), preferred_element_type=jn...  35.2 us
    dot_general x4, matrix products, shards(): up_act = jnp.dot(block, up_rel, preferred_element_type=jnp.float32)  31.8 us
  transfers between devices with their start and end apart: 34, of which 15 were waited for; matrix products, arithmetic and copies ran while one was open for 20% of the time, Pallas kernels for 0%

profile of v1, /device:TPU:0, one launch (start us, length us, event | category | flops | bytes accessed | tf_op | source)
XLA Modules:
  0.0 943.4 jit_solution(6029346725731031763)
XLA Ops:
  0.6 7.9 copy.36
  16.2 7.8 fusion.5
  41.2 35.9 %collective-permute-done = bf16[960,1024]{1,0:T(8,128)(2,1)} collective-permute-done((bf16[960,1024]{1,0:T(8,128)(2,1)}, bf16[960,1024]{1,0:T(8,128)(2,1)}, u32[]{:S(2)}, u32[]{:S(2)}) %collective-permute-start) | collective-permute-done | bytes 1966112 | tf_op jit(solution)/shard_map/ppermute | solution.py:42
  82.0 35.9 %collective-permute-done.10 = bf16[960,1024]{1,0:T(8,128)(2,1)} collective-permute-done((bf16[960,1024]{1,0:T(8,128)(2,1)}, bf16[960,1024]{1,0:T(8,128)(2,1)}, u32[]{:S(2)}, u32[]{:S(2)}) %collective-permute-start.10) | collective-permute-done | bytes 1966112 | tf_op jit(solution)/shard_map/ppermute | solution.py:42
  122.5 80.1 %collective-permute-done.17 = bf16[960,1024]{1,0:T(8,128)(2,1)} collective-permute-done((bf16[960,1024]{1,0:T(8,128)(2,1)}, bf16[960,1024]{1,0:T(8,128)(2,1)}, u32[]{:S(2)}, u32[]{:S(2)}) %collective-permute-start.17) | collective-permute-done | bytes 1966112 | tf_op jit(solution)/shard_map/ppermute | solution.py:42
  217.3 34.3 %collective-permute-done.11 = bf16[960,1024]{1,0:T(8,128)(2,1)} collective-permute-done((bf16[960,1024]{1,0:T(8,128)(2,1)}, bf16[960,1024]{1,0:T(8,128)(2,1)}, u32[]{:S(2)}, u32[]{:S(2)}) %collective-permute-start.11) | collective-permute-done | bytes 1966112 | tf_op jit(solution)/shard_map/ppermute | solution.py:54
  265.2 28.1 %collective-permute-done.18 = bf16[960,1024]{1,0:T(8,128)(2,1)S(1)} collective-permute-done((bf16[960,1024]{1,0:T(8,128)(2,1)}, bf16[960,1024]{1,0:T(8,128)(2,1)S(1)}, u32[]{:S(2)}, u32[]{:S(2)}) %collective-permute-start.18) | collective-permute-done | bytes 1966112 | tf_op jit(solution)/shard_map/ppermute | solution.py:54
  306.4 7.6 fusion.51
  314.1 8.3 multiply_convert_fusion.3
  335.6 7.7 multiply_convert_fusion.2
  356.9 7.9 multiply_convert_fusion.1
  369.0 7.9 multiply_convert_fusion
  408.3 24.2 %collective-permute-done.8 = bf16[960,1024]{1,0:T(8,128)(2,1)} collective-permute-done((bf16[960,1024]{1,0:T(8,128)(2,1)S(1)}, bf16[960,1024]{1,0:T(8,128)(2,1)}, u32[]{:S(2)}, u32[]{:S(2)}) %collective-permute-start.8) | collective-permute-done | bytes 1966112 | tf_op jit(solution)/shard_map/ppermute | solution.py:54
  436.5 38.1 %collective-permute-done.15 = bf16[960,1024]{1,0:T(8,128)(2,1)} collective-permute-done((bf16[960,1024]{1,0:T(8,128)(2,1)S(1)}, bf16[960,1024]{1,0:T(8,128)(2,1)}, u32[]{:S(2)}, u32[]{:S(2)}) %collective-permute-start.15) | collective-permute-done | bytes 1966112 | tf_op jit(solution)/shard_map/ppermute | solution.py:54
  477.0 39.7 %collective-permute-done.22 = bf16[960,1024]{1,0:T(8,128)(2,1)} collective-permute-done((bf16[960,1024]{1,0:T(8,128)(2,1)}, bf16[960,1024]{1,0:T(8,128)(2,1)}, u32[]{:S(2)}, u32[]{:S(2)}) %collective-permute-start.22) | collective-permute-done | bytes 1966112 | tf_op jit(solution)/shard_map/ppermute | solution.py:54
  519.2 38.8 %collective-permute-done.25 = bf16[960,1024]{1,0:T(8,128)(2,1)} collective-permute-done((bf16[960,1024]{1,0:T(8,128)(2,1)}, bf16[960,1024]{1,0:T(8,128)(2,1)}, u32[]{:S(2)}, u32[]{:S(2)}) %collective-permute-start.25) | collective-permute-done | bytes 1966112 | tf_op jit(solution)/shard_map/ppermute | solution.py:54
  560.5 45.6 %collective-permute-done.23 = bf16[960,1024]{1,0:T(8,128)(2,1)S(1)} collective-permute-done((bf16[960,1024]{1,0:T(8,128)(2,1)S(1)}, bf16[960,1024]{1,0:T(8,128)(2,1)S(1)}, u32[]{:S(2)}, u32[]{:S(2)}) %collective-permute-start.23) | collective-permute-done | bytes 1966112 | tf_op jit(solution)/shard_map/ppermute | solution.py:42
  620.7 42.1 %collective-permute-done.27 = bf16[240,4096]{1,0:T(8,128)(2,1)} collective-permute-done((bf16[240,4096]{1,0:T(8,128)(2,1)}, bf16[240,4096]{1,0:T(8,128)(2,1)}, u32[]{:S(2)}, u32[]{:S(2)}) %collective-permute-start.27) | collective-permute-done | bytes 1966112 | tf_op jit(solution)/shard_map/ppermute | solution.py:42
  664.3 10.0 %scatter_custom_fusion = s32[1920]{0:T(1024)S(1)} fusion(s32[1920]{0:T(1024)S(1)} %get-tuple-element.23, s32[1920]{0:T(1024)S(1)} %get-tuple-element.24, s32[]{:T(128)} %constant.220.clone.1), kind=kCustom, calls=%fused_computation.148 | custom fusion | bytes 7684 | tf_op jit(solution)/shard_map/scatter | solution.py:143
  674.5 71.6 %collective-permute-done.29 = bf16[240,4096]{1,0:T(8,128)(2,1)} collective-permute-done((bf16[240,4096]{1,0:T(8,128)(2,1)}, bf16[240,4096]{1,0:T(8,128)(2,1)}, u32[]{:S(2)}, u32[]{:S(2)}) %collective-permute-start.29) | collective-permute-done | bytes 1966112 | tf_op jit(solution)/shard_map/ppermute | solution.py:42
  763.3 28.8 %collective-permute-done.30 = bf16[240,4096]{1,0:T(8,128)(2,1)S(1)} collective-permute-done((bf16[240,4096]{1,0:T(8,128)(2,1)}, bf16[240,4096]{1,0:T(8,128)(2,1)S(1)}, u32[]{:S(2)}, u32[]{:S(2)}) %collective-permute-start.30) | collective-permute-done | bytes 1966112 | tf_op jit(solution)/shard_map/ppermute | solution.py:50
  796.0 35.4 %collective-permute-done.32 = bf16[240,4096]{1,0:T(8,128)(2,1)S(1)} collective-permute-done((bf16[240,4096]{1,0:T(8,128)(2,1)}, bf16[240,4096]{1,0:T(8,128)(2,1)S(1)}, u32[]{:S(2)}, u32[]{:S(2)}) %collective-permute-start.32) | collective-permute-done | bytes 1966112 | tf_op jit(solution)/shard_map/ppermute | solution.py:50
  843.4 43.9 %all-to-all-start = ((bf16[32,60,512]{2,1,0:T(8,128)(2,1)}), bf16[32,60,512]{2,1,0:T(8,128)(2,1)S(1)}, u32[]{:S(2)}, u32[]{:S(2)}) async-start(bf16[32,60,512]{2,1,0:T(8,128)(2,1)} %broadcast_select_fusion), calls=%async_computation | async-start | bytes 4194304 | tf_op jit(solution)/shard_map/all_to_all | solution.py:155
  891.0 45.1 %all-to-all-done = bf16[32,60,512]{2,1,0:T(8,128)(2,1)S(1)} async-done(((bf16[32,60,512]{2,1,0:T(8,128)(2,1)}), bf16[32,60,512]{2,1,0:T(8,128)(2,1)S(1)}, u32[]{:S(2)}, u32[]{:S(2)}) %all-to-all-start) | async-done | bytes 1966112 | tf_op jit(solution)/shard_map/all_to_all | solution.py:155
  (196 shorter events, 208.5 us)
Async XLA Ops:
  31.1 86.9 %collective-permute-start.10 = (bf16[960,1024]{1,0:T(8,128)(2,1)}, bf16[960,1024]{1,0:T(8,128)(2,1)}, u32[]{:S(2)}, u32[]{:S(2)}) collective-permute-start(bf16[960,1024]{1,0:T(8,128)(2,1)} %get-tuple-element.4), channel_id=1, source_target_pairs={{0,24},{4,28},{8,0},{12,4},{16,8},{20,12},{24,16},{28,20},{1,25},{... | collective-permute-start | bytes 5898248 | tf_op jit(solution)/shard_map/ppermute | solution.py:42
  33.3 169.3 %collective-permute-start.17 = (bf16[960,1024]{1,0:T(8,128)(2,1)}, bf16[960,1024]{1,0:T(8,128)(2,1)}, u32[]{:S(2)}, u32[]{:S(2)}) collective-permute-start(bf16[960,1024]{1,0:T(8,128)(2,1)} %get-tuple-element.4), channel_id=1, source_target_pairs={{0,16},{4,20},{8,24},{12,28},{16,0},{20,4},{24,8},{28,12},{1,17},{... | collective-permute-start | bytes 5898248 | tf_op jit(solution)/shard_map/ppermute | solution.py:42
  34.3 171.4 %collective-permute-start.4 = (bf16[4096,256]{1,0:T(8,128)(2,1)}, bf16[4096,256]{1,0:T(8,128)(2,1)}, u32[]{:S(2)}, u32[]{:S(2)}) collective-permute-start(bf16[4096,256]{1,0:T(8,128)(2,1)} %param.13), channel_id=1, source_target_pairs={{0,4},{4,0},{8,12},{12,8},{16,20},{20,16},{24,28},{28,24},{1,5},{5... | collective-permute-start | bytes 6291464 | tf_op jit(solution)/shard_map/ppermute | solution.py:50
  35.8 173.2 %collective-permute-start.5 = (bf16[4096,256]{1,0:T(8,128)(2,1)}, bf16[4096,256]{1,0:T(8,128)(2,1)}, u32[]{:S(2)}, u32[]{:S(2)}) collective-permute-start(bf16[4096,256]{1,0:T(8,128)(2,1)} %param.14), channel_id=1, source_target_pairs={{0,4},{4,0},{8,12},{12,8},{16,20},{20,16},{24,28},{28,24},{1,5},{5... | collective-permute-start | bytes 6291464 | tf_op jit(solution)/shard_map/ppermute | solution.py:50
  77.1 137.3 %collective-permute-start.6 = (bf16[4096,256]{1,0:T(8,128)(2,1)S(1)}, bf16[4096,256]{1,0:T(8,128)(2,1)S(1)}, u32[]{:S(2)}, u32[]{:S(2)}) collective-permute-start(bf16[4096,256]{1,0:T(8,128)(2,1)S(1)} %copy-done.3), channel_id=1, source_target_pairs={{0,4},{4,0},{8,12},{12,8},{16,20},{20,16},{24,28},{28,24},{1,5},{5... | collective-permute-start | bytes 6291464 | tf_op jit(solution)/shard_map/ppermute | solution.py:50
  118.0 99.3 %collective-permute-start.1 = (bf16[960,1024]{1,0:T(8,128)(2,1)}, bf16[960,1024]{1,0:T(8,128)(2,1)}, u32[]{:S(2)}, u32[]{:S(2)}) collective-permute-start(bf16[960,1024]{1,0:T(8,128)(2,1)} %collective-permute-done), channel_id=1, source_target_pairs={{0,2},{1,3},{2,0},{3,1},{4,6},{5,7},{6,4},{7,5},{8,10},{9,11},{10,... | collective-permute-start | bytes 5898248 | tf_op jit(solution)/shard_map/ppermute | solution.py:54
  202.6 92.2 %collective-permute-start.2 = (bf16[960,1024]{1,0:T(8,128)(2,1)}, bf16[960,1024]{1,0:T(8,128)(2,1)}, u32[]{:S(2)}, u32[]{:S(2)}) collective-permute-start(bf16[960,1024]{1,0:T(8,128)(2,1)} %collective-permute-done), channel_id=1, source_target_pairs={{0,1},{1,0},{2,3},{3,2},{4,5},{5,4},{6,7},{7,6},{8,9},{9,8},{10,11... | collective-permute-start | bytes 5898248 | tf_op jit(solution)/shard_map/ppermute | solution.py:57
  209.0 89.4 %collective-permute-start.12 = (bf16[960,1024]{1,0:T(8,128)(2,1)}, bf16[960,1024]{1,0:T(8,128)(2,1)}, u32[]{:S(2)}, u32[]{:S(2)}) collective-permute-start(bf16[960,1024]{1,0:T(8,128)(2,1)} %collective-permute-done.10), channel_id=1, source_target_pairs={{0,1},{1,0},{2,3},{3,2},{4,5},{5,4},{6,7},{7,6},{8,9},{9,8},{10,11... | collective-permute-start | bytes 5898248 | tf_op jit(solution)/shard_map/ppermute | solution.py:57
  214.4 78.9 %collective-permute-start.18 = (bf16[960,1024]{1,0:T(8,128)(2,1)}, bf16[960,1024]{1,0:T(8,128)(2,1)S(1)}, u32[]{:S(2)}, u32[]{:S(2)}) collective-permute-start(bf16[960,1024]{1,0:T(8,128)(2,1)} %collective-permute-done.17), channel_id=1, source_target_pairs={{0,2},{1,3},{2,0},{3,1},{4,6},{5,7},{6,4},{7,5},{8,10},{9,11},{10,... | collective-permute-start | bytes 5898248 | tf_op jit(solution)/shard_map/ppermute | solution.py:54
  217.3 84.1 %collective-permute-start.19 = (bf16[960,1024]{1,0:T(8,128)(2,1)}, bf16[960,1024]{1,0:T(8,128)(2,1)S(1)}, u32[]{:S(2)}, u32[]{:S(2)}) collective-permute-start(bf16[960,1024]{1,0:T(8,128)(2,1)} %collective-permute-done.17), channel_id=1, source_target_pairs={{0,1},{1,0},{2,3},{3,2},{4,5},{5,4},{6,7},{7,6},{8,9},{9,8},{10,11... | collective-permute-start | bytes 5898248 | tf_op jit(solution)/shard_map/ppermute | solution.py:57
  294.8 53.1 %collective-permute-start.20 = (bf16[960,1024]{1,0:T(8,128)(2,1)S(1)}, bf16[960,1024]{1,0:T(8,128)(2,1)S(1)}, u32[]{:S(2)}, u32[]{:S(2)}) collective-permute-start(bf16[960,1024]{1,0:T(8,128)(2,1)S(1)} %collective-permute-done.18), channel_id=1, source_target_pairs={{0,1},{1,0},{2,3},{3,2},{4,5},{5,4},{6,7},{7,6},{8,9},{9,8},{10,11... | collective-permute-start | bytes 5898248 | tf_op jit(solution)/shard_map/ppermute | solution.py:57
  326.6 55.1 %collective-permute-start.7 = (bf16[960,2048]{1,0:T(8,128)(2,1)}, bf16[960,2048]{1,0:T(8,128)(2,1)}, u32[]{:S(2)}, u32[]{:S(2)}) collective-permute-start(bf16[960,2048]{1,0:T(8,128)(2,1)} %convolution_convert_fusion.3), channel_id=1, source_target_pairs={{0,1},{1,0},{2,3},{3,2},{4,5},{5,4},{6,7},{7,6},{8,9},{9,8},{10,11... | collective-permute-start | bytes 11796488 | tf_op jit(solution)/shard_map/ppermute | solution.py:57
  393.1 81.5 %collective-permute-start.15 = (bf16[960,1024]{1,0:T(8,128)(2,1)S(1)}, bf16[960,1024]{1,0:T(8,128)(2,1)}, u32[]{:S(2)}, u32[]{:S(2)}) collective-permute-start(bf16[960,1024]{1,0:T(8,128)(2,1)S(1)} %slice.72), channel_id=1, source_target_pairs={{0,2},{1,3},{2,0},{3,1},{4,6},{5,7},{6,4},{7,5},{8,10},{9,11},{10,... | collective-permute-start | bytes 5898248 | tf_op jit(solution)/shard_map/ppermute | solution.py:54
  399.7 117.0 %collective-permute-start.22 = (bf16[960,1024]{1,0:T(8,128)(2,1)}, bf16[960,1024]{1,0:T(8,128)(2,1)}, u32[]{:S(2)}, u32[]{:S(2)}) collective-permute-start(bf16[960,1024]{1,0:T(8,128)(2,1)} %slice.71), channel_id=1, source_target_pairs={{0,2},{1,3},{2,0},{3,1},{4,6},{5,7},{6,4},{7,5},{8,10},{9,11},{10,... | collective-permute-start | bytes 5898248 | tf_op jit(solution)/shard_map/ppermute | solution.py:54
  407.8 150.2 %collective-permute-start.25 = (bf16[960,1024]{1,0:T(8,128)(2,1)}, bf16[960,1024]{1,0:T(8,128)(2,1)}, u32[]{:S(2)}, u32[]{:S(2)}) collective-permute-start(bf16[960,1024]{1,0:T(8,128)(2,1)} %slice.70), channel_id=1, source_target_pairs={{0,2},{1,3},{2,0},{3,1},{4,6},{5,7},{6,4},{7,5},{8,10},{9,11},{10,... | collective-permute-start | bytes 5898248 | tf_op jit(solution)/shard_map/ppermute | solution.py:54
  434.8 123.1 %collective-permute-start.9 = (bf16[960,1024]{1,0:T(8,128)(2,1)S(1)}, bf16[960,1024]{1,0:T(8,128)(2,1)S(1)}, u32[]{:S(2)}, u32[]{:S(2)}) collective-permute-start(bf16[960,1024]{1,0:T(8,128)(2,1)S(1)} %fusion.12), channel_id=1, source_target_pairs={{0,24},{4,28},{8,0},{12,4},{16,8},{20,12},{24,16},{28,20},{1,25},{... | collective-permute-start | bytes 5898248 | tf_op jit(solution)/shard_map/ppermute | solution.py:42
  477.0 81.0 %collective-permute-start.16 = (bf16[960,1024]{1,0:T(8,128)(2,1)S(1)}, bf16[960,1024]{1,0:T(8,128)(2,1)S(1)}, u32[]{:S(2)}, u32[]{:S(2)}) collective-permute-start(bf16[960,1024]{1,0:T(8,128)(2,1)S(1)} %fusion.11), channel_id=1, source_target_pairs={{0,8},{4,12},{8,16},{12,20},{16,24},{20,28},{24,0},{28,4},{1,9},{5... | collective-permute-start | bytes 5898248 | tf_op jit(solution)/shard_map/ppermute | solution.py:42
  519.1 87.0 %collective-permute-start.23 = (bf16[960,1024]{1,0:T(8,128)(2,1)S(1)}, bf16[960,1024]{1,0:T(8,128)(2,1)S(1)}, u32[]{:S(2)}, u32[]{:S(2)}) collective-permute-start(bf16[960,1024]{1,0:T(8,128)(2,1)S(1)} %fusion.10), channel_id=1, source_target_pairs={{0,16},{4,20},{8,24},{12,28},{16,0},{20,4},{24,8},{28,12},{1,17},{... | collective-permute-start | bytes 5898248 | tf_op jit(solution)/shard_map/ppermute | solution.py:42
  614.9 131.2 %collective-permute-start.29 = (bf16[240,4096]{1,0:T(8,128)(2,1)}, bf16[240,4096]{1,0:T(8,128)(2,1)}, u32[]{:S(2)}, u32[]{:S(2)}) collective-permute-start(bf16[240,4096]{1,0:T(8,128)(2,1)} %reshape.78), channel_id=1, source_target_pairs={{0,16},{4,20},{8,24},{12,28},{16,0},{20,4},{24,8},{28,12},{1,17},{... | collective-permute-start | bytes 5898248 | tf_op jit(solution)/shard_map/ppermute | solution.py:42
  617.0 134.5 %collective-permute-start.31 = (bf16[240,4096]{1,0:T(8,128)(2,1)}, bf16[240,4096]{1,0:T(8,128)(2,1)}, u32[]{:S(2)}, u32[]{:S(2)}) collective-permute-start(bf16[240,4096]{1,0:T(8,128)(2,1)} %reshape.78), channel_id=1, source_target_pairs={{0,24},{4,28},{8,0},{12,4},{16,8},{20,12},{24,16},{28,20},{1,25},{... | collective-permute-start | bytes 5898248 | tf_op jit(solution)/shard_map/ppermute | solution.py:42
  618.9 133.2 %collective-permute-start.26 = (bf16[240,4096]{1,0:T(8,128)(2,1)}, bf16[240,4096]{1,0:T(8,128)(2,1)}, u32[]{:S(2)}, u32[]{:S(2)}) collective-permute-start(bf16[240,4096]{1,0:T(8,128)(2,1)} %reshape.78), channel_id=1, source_target_pairs={{0,4},{4,0},{8,12},{12,8},{16,20},{20,16},{24,28},{28,24},{1,5},{5... | collective-permute-start | bytes 5898248 | tf_op jit(solution)/shard_map/ppermute | solution.py:50
  662.8 94.9 %collective-permute-start.28 = (bf16[240,4096]{1,0:T(8,128)(2,1)}, bf16[240,4096]{1,0:T(8,128)(2,1)}, u32[]{:S(2)}, u32[]{:S(2)}) collective-permute-start(bf16[240,4096]{1,0:T(8,128)(2,1)} %collective-permute-done.27), channel_id=1, source_target_pairs={{0,4},{4,0},{8,12},{12,8},{16,20},{20,16},{24,28},{28,24},{1,5},{5... | collective-permute-start | bytes 5898248 | tf_op jit(solution)/shard_map/ppermute | solution.py:50
  751.5 79.9 %collective-permute-start.32 = (bf16[240,4096]{1,0:T(8,128)(2,1)}, bf16[240,4096]{1,0:T(8,128)(2,1)S(1)}, u32[]{:S(2)}, u32[]{:S(2)}) collective-permute-start(bf16[240,4096]{1,0:T(8,128)(2,1)} %collective-permute-done.31), channel_id=1, source_target_pairs={{0,4},{4,0},{8,12},{12,8},{16,20},{20,16},{24,28},{28,24},{1,5},{5... | collective-permute-start | bytes 5898248 | tf_op jit(solution)/shard_map/ppermute | solution.py:50
  843.4 92.6 %all-to-all-start = ((bf16[32,60,512]{2,1,0:T(8,128)(2,1)}), bf16[32,60,512]{2,1,0:T(8,128)(2,1)S(1)}, u32[]{:S(2)}, u32[]{:S(2)}) async-start(bf16[32,60,512]{2,1,0:T(8,128)(2,1)} %broadcast_select_fusion), calls=%async_computation | async-start | bytes 4194304 | tf_op jit(solution)/shard_map/all_to_all | solution.py:155
  (44 other events, 1328.0 us)

commit v2 on v1

--- a/solution.py
+++ b/solution.py
@@ -33,11 +33,9 @@
     far, near = req_index // near_count, req_index % near_count
     pair, core = mlp_index // 2, mlp_index % 2
 
-    def shift_far(x, s):
+    def swap_far(x, k):
         perm = [
-            (f * near_count + n, ((f + s) % far_count) * near_count + n)
-            for f in range(far_count)
-            for n in range(near_count)
+            (f * near_count + n, (f ^ k) * near_count + n) for f in range(far_count) for n in range(near_count)
         ]
         return lax.ppermute(x, "req", perm)
 
@@ -59,9 +57,6 @@
     rows_here, model_width = patches.shape
     feat_width = model_width // mlp_count
 
-    def with_near(w):
-        return jnp.concatenate([w] + [shift_near(w, s) for s in range(1, near_count)], axis=1)
-
     def quarter_at(t, d, sign):
         other = (pair + sign * t) % pair_count
         return (other * 2 + (core + d) % 2) * feat_width
@@ -71,48 +66,70 @@
             [lax.dynamic_slice_in_dim(x, quarter_at(t, d, sign), feat_width, axis=axis) for t, d in which], axis=axis
         )
 
-    both = [(t, d) for d in range(2) for t in range(pair_count)]
     kept = [(t, 0) for t in range(pair_count)]
     sent = [(t, 1) for t in range(pair_count)]
+
+    weights = jnp.concatenate([gate_weight, up_weight, down_weight], axis=1)
+    from_near = [shift_near(weights, s) for s in range(1, near_count)]
+    units = gate_weight.shape[1]
 
     inputs = patches.astype(jnp.float32)
     normed = layer_norm(inputs, norm_gain, norm_bias).astype(jnp.bfloat16)
     own_quarter = lax.dynamic_slice_in_dim(normed, mlp_index * feat_width, feat_width, axis=1)
-    gate_full = with_near(gate_weight)
-    up_full = with_near(up_weight)
-    down_full = with_near(down_weight)
-    gate_rel = relative(gate_full, 0, -1, both)
-    up_rel = relative(up_full, 0, -1, both)
+
+    quarters = {1: swap_far(own_quarter, 1), 2: swap_far(own_quarter, 2)}
+    quarters[1], text_rows = lax.optimization_barrier((quarters[1], text_rows))
+    quarters[3] = swap_far(quarters[2], 1)
+    halves = {0: (relative(normed, 1, -1, kept), relative(normed, 1, -1, sent))}
+    for k in (1, 2, 3):
+        first = quarters[k]
+        column = jnp.concatenate([first] + [shift_pair(first, t) for t in range(1, pair_count)], axis=1)
+        halves[k] = (column, swap_core(column))
+
+    def with_near(index):
+        cut = slice(index * units, (index + 1) * units)
+        return jnp.concatenate([w[:, cut] for w in [weights] + from_near], axis=1)
+
+    gate_full, up_full, down_full = with_near(0), with_near(1), with_near(2)
+    gate_rel = [relative(gate_full, 0, -1, which) for which in (kept, sent)]
+    up_rel = [relative(up_full, 0, -1, which) for which in (kept, sent)]
+    down_kept = relative(down_full, 0, 1, kept)
     down_sent = relative(down_full, 0, 1, sent)
-    down_kept = relative(down_full, 0, 1, kept)
-
-    def normed_block(s):
-        if s == 0:
-            return relative(normed, 1, -1, both)
-        first = shift_far(own_quarter, s)
-        column = [first] + [shift_pair(first, t) for t in range(1, pair_count)]
-        return jnp.concatenate(column + [swap_core(c) for c in column], axis=1)
-
-    blocks = [normed_block(s) for s in range(far_count)]
+
+    def dot(a, w):
+        return jnp.dot(a, w, preferred_element_type=jnp.float32)
 
     def dot_t(a, w):
         return lax.dot_general(a, w, (((1,), (1,)), ((), ())), preferred_element_type=jnp.float32)
 
-    total = None
-    for s in (1, 3, 2, 0):
-        block = blocks[s]
-        gate_act = jnp.dot(block, gate_rel, preferred_element_type=jnp.float32)
-        up_act = jnp.dot(block, up_rel, preferred_element_type=jnp.float32)
-        hidden = (jax.nn.silu(gate_act) * up_act).astype(jnp.bfloat16)
-        from_core = swap_core(dot_t(hidden, down_sent).astype(jnp.bfloat16))
-        of_core = dot_t(hidden, down_kept) + from_core.astype(jnp.float32)
+    hiddens, from_core, after = {}, {}, None
+    for k in (0, 1, 2, 3):
+        here, there = halves[k]
+        if after is not None:
+            here, there, _ = lax.optimization_barrier((here, there, after))
+        if k >= 2:
+            here, there, from_core[k - 2] = lax.optimization_barrier((here, there, from_core[k - 2]))
+        gate_act = dot(here, gate_rel[0]) + dot(there, gate_rel[1])
+        up_act = dot(here, up_rel[0]) + dot(there, up_rel[1])
+        hiddens[k] = (jax.nn.silu(gate_act) * up_act).astype(jnp.bfloat16)
+        after = dot_t(hiddens[k], down_sent).astype(jnp.bfloat16)
+        from_core[k] = swap_core(after)
+
+    def over_mlp(k):
+        of_core = dot_t(hiddens[k], down_kept) + from_core[k].astype(jnp.float32)
         mine = of_core[:, :feat_width]
         for t in range(1, pair_count):
             part = of_core[:, t * feat_width : (t + 1) * feat_width].astype(jnp.bfloat16)
             mine = mine + shift_pair(part, t).astype(jnp.float32)
-        if s:
-            mine = shift_far(mine.astype(jnp.bfloat16), far_count - s).astype(jnp.float32)
-        total = mine if total is None else total + mine
+        return mine
+
+    def sent_far(x, k):
+        return swap_far(x.astype(jnp.bfloat16), k).astype(jnp.float32)
+
+    total = over_mlp(0)
+    farthest = sent_far(over_mlp(3), 1)
+    total = total + sent_far(over_mlp(2) + farthest, 2)
+    total = total + sent_far(over_mlp(1), 1)
 
     scale_here = lax.dynamic_slice_in_dim(layer_scale, mlp_index * feat_width, feat_width)
     own_inputs = lax.dynamic_slice_in_dim(patches, mlp_index * feat_width, feat_width, axis=1).astype(jnp.float32)
@@ -132,31 +149,38 @@
     first_off = jnp.min(jnp.where(bucket_hit, offsets[:, None], piece_rows), axis=0)
     counts = jnp.sum(bucket_hit.astype(jnp.int32), axis=0)
     slot_first = jnp.sum(jnp.where(bucket_hit, first_off[None, :], 0), axis=1)
-    rows_at = piece_ids * capacity + offsets - slot_first
+    piece_req, piece_mlp = piece_ids // mlp_count, piece_ids % mlp_count
+    rel_core = (piece_mlp % 2 - core) % 2
+    rel_pair = (piece_mlp // 2 - pair) % pair_count
+    rel_piece = (rel_core * pair_count + rel_pair) * req_count + piece_req
+    rows_at = rel_piece * capacity + offsets - slot_first
     rows_at = jnp.where(is_valid, rows_at, bucket_count * capacity)
     slot_ids = jnp.arange(slot_count, dtype=jnp.int32)
     slot_req = slot_ids // slots_here
-    slot_far = (far - slot_req // near_count) % far_count
+    slot_far = jnp.bitwise_xor(far, slot_req // near_count)
     slot_near = (near - slot_req % near_count) % near_count
     slot_place = (slot_far * near_count + slot_near) * slots_here + slot_ids % slots_here
     sources = (
         jnp.zeros((bucket_count * capacity,), jnp.int32).at[rows_at].set(slot_place, mode="drop")
     )
 
+    firsts = {0: merged, 1: swap_far(merged, 1), 2: swap_far(merged, 2)}
+    firsts[3] = swap_far(firsts[2], 1)
     gathered = []
-    for s in range(far_count):
-        first = merged if s == 0 else shift_far(merged, s)
-        gathered += [first] + [shift_near(first, t) for t in range(1, near_count)]
-    products = jnp.concatenate(
-        [jnp.dot(g, weight_cols, preferred_element_type=jnp.float32).astype(jnp.bfloat16) for g in gathered], axis=0
-    )
+    for k in range(far_count):
+        gathered += [firsts[k]] + [shift_near(firsts[k], t) for t in range(1, near_count)]
+    products = jnp.concatenate([dot(g, weight_cols).astype(jnp.bfloat16) for g in gathered], axis=0)
     picked = jnp.take(products, sources, axis=0)
     out_width = picked.shape[1]
+    half = picked.shape[0] // 2
+    core_sum = picked[:half].astype(jnp.float32) + swap_core(picked[half:]).astype(jnp.float32)
+    core_sum = core_sum.reshape(pair_count, req_count * capacity, out_width)
+    summed = core_sum[0]
+    for t in range(1, pair_count):
+        summed = summed + shift_pair(core_sum[t].astype(jnp.bfloat16), t).astype(jnp.float32)
     arrived = lax.all_to_all(
-        picked.reshape(bucket_count, capacity, out_width), ("req", "mlp"), split_axis=0, concat_axis=0, tiled=True
+        summed.astype(jnp.bfloat16), "req", split_axis=0, concat_axis=1, tiled=True
     )
-    arrived = arrived.reshape(req_count, mlp_count, capacity, out_width).astype(jnp.float32).sum(axis=1)
-    arrived = arrived.astype(jnp.bfloat16).transpose(1, 0, 2).reshape(capacity, req_count * out_width)
 
     bucket_here = req_index * mlp_count + mlp_index
     start_here = first_off[bucket_here]

time: 952 us -> 831 us (0.87)
  waiting for transfers between devices: 624 us -> 579 us
  starting transfers between devices: 74.4 us -> 30.8 us
  local copies, waits for them, and re-layouts: 92.9 us -> 62.2 us
    ppermute x9, waiting for transfers between devices: 311 us -> 238 us  [swap_far(): return lax.ppermute(x, 'req', perm)]
    ppermute x7 -> x8, waiting for transfers between devices: 203 us -> 245 us  [shift_pair(): return lax.ppermute(x, 'mlp', perm)]
    all_to_all x1, starting transfers between devices: 43.9 us -> 3.49 us  [shards(): lax.all_to_all(summed.astype(jnp.bfloat16), 'req', split_axis=0, concat_a...]
    all_to_all x1, waiting for transfers between devices: 45.1 us -> 10.3 us  [shards(): lax.all_to_all(summed.astype(jnp.bfloat16), 'req', split_axis=0, concat_a...]
    unnamed x81 -> x49, local copies, waits for them, and re-layouts: 41.1 us -> 12.7 us
    ppermute x10 -> x8, waiting for transfers between devices: 0.03 us -> 13.7 us  [swap_core(): return lax.ppermute(x, 'mlp', [(m, m ^ 1) for m in range(mlp_count)])]
    ppermute x7 -> x5, waiting for transfers between devices: 64.2 us -> 71.8 us  [shift_near(): return lax.ppermute(x, 'req', perm)]
    dot_general x16 -> x24, matrix products: 81.9 us -> 84.1 us  [dot(): return jnp.dot(a, w, preferred_element_type=jnp.float32)]
  transfers between devices with their start and end apart: 34 -> 31, of which waited for: 15 -> 18; matrix products, arithmetic and copies ran while one was open for 20% -> 18% of each run, Pallas kernels for 0% -> 0%
where the time goes in v2:
time: 831 us; the launch traced here: 820 us
  waiting for transfers between devices  579 us (70%)
  matrix products  111 us (13%)
  local copies, waits for them, and re-layouts  62.2 us (7%)
  other arithmetic  35.8 us (4%)
  starting transfers between devices  30.8 us (4%)
    ppermute x8, waiting for transfers between devices, shift_pair(): return lax.ppermute(x, 'mlp', perm)  245 us
    ppermute x9, waiting for transfers between devices, swap_far(): return lax.ppermute(x, 'req', perm)  238 us
    dot_general x24, matrix products, dot(): return jnp.dot(a, w, preferred_element_type=jnp.float32)  84.1 us
    ppermute x5, waiting for transfers between devices, shift_near(): return lax.ppermute(x, 'req', perm)  71.8 us
    dot_general x8, matrix products, dot_t(): lax.dot_general(a, w, (((1,), (1,)), ((), ())), preferred_element_type=jn...  26.5 us
  transfers between devices with their start and end apart: 31, of which 18 were waited for; matrix products, arithmetic and copies ran while one was open for 18% of the time, Pallas kernels for 0%

profile of v2, /device:TPU:0, one launch (start us, length us, event | category | flops | bytes accessed | tf_op | source)
XLA Modules:
  0.0 820.5 jit_solution(2196422362581777125)
XLA Ops:
  0.7 8.0 copy.28
  22.4 7.8 fusion.5
  38.0 82.2 %collective-permute-done.4 = bf16[960,1024]{1,0:T(8,128)(2,1)} collective-permute-done((bf16[960,1024]{1,0:T(8,128)(2,1)S(1)}, bf16[960,1024]{1,0:T(8,128)(2,1)}, u32[]{:S(2)}, u32[]{:S(2)}) %collective-permute-start.4) | collective-permute-done | bytes 1966112 | tf_op jit(solution)/shard_map/ppermute | solution.py:40
  130.6 35.7 %collective-permute-done.5 = bf16[960,1024]{1,0:T(8,128)(2,1)} collective-permute-done((bf16[960,1024]{1,0:T(8,128)(2,1)}, bf16[960,1024]{1,0:T(8,128)(2,1)}, u32[]{:S(2)}, u32[]{:S(2)}) %collective-permute-start.5) | collective-permute-done | bytes 1966112 | tf_op jit(solution)/shard_map/ppermute | solution.py:52
  169.4 36.7 %collective-permute-done.2 = bf16[960,1024]{1,0:T(8,128)(2,1)} collective-permute-done((bf16[960,1024]{1,0:T(8,128)(2,1)}, bf16[960,1024]{1,0:T(8,128)(2,1)}, u32[]{:S(2)}, u32[]{:S(2)}) %collective-permute-start.2) | collective-permute-done | bytes 1966112 | tf_op jit(solution)/shard_map/ppermute | solution.py:52
  238.7 15.7 %collective-permute-done.12 = bf16[960,1024]{1,0:T(8,128)(2,1)S(1)} collective-permute-done((bf16[960,1024]{1,0:T(8,128)(2,1)S(1)}, bf16[960,1024]{1,0:T(8,128)(2,1)S(1)}, u32[]{:S(2)}, u32[]{:S(2)}) %collective-permute-start.12) | collective-permute-done | bytes 1966112 | tf_op jit(solution)/shard_map/ppermute | solution.py:52
  267.6 4.8 multiply_convert_fusion.2
  277.0 5.7 fusion.90
  314.6 11.1 %collective-permute-done.15 = bf16[960,2048]{1,0:T(8,128)(2,1)S(1)} collective-permute-done((bf16[960,2048]{1,0:T(8,128)(2,1)S(1)}, bf16[960,2048]{1,0:T(8,128)(2,1)S(1)}, u32[]{:S(2)}, u32[]{:S(2)}) %collective-permute-start.15) | collective-permute-done | bytes 3932192 | tf_op jit(solution)/shard_map/ppermute | solution.py:55
  333.0 4.6 convert_add_fusion.2
  339.6 34.4 %collective-permute-done.16 = bf16[960,1024]{1,0:T(8,128)(2,1)S(1)} collective-permute-done((bf16[960,1024]{1,0:T(8,128)(2,1)S(1)}, bf16[960,1024]{1,0:T(8,128)(2,1)S(1)}, u32[]{:S(2)}, u32[]{:S(2)}) %collective-permute-start.16) | collective-permute-done | bytes 1966112 | tf_op jit(solution)/shard_map/ppermute | solution.py:52
  376.5 4.7 convert_add_fusion.3
  383.1 33.1 %collective-permute-done.19 = bf16[960,1024]{1,0:T(8,128)(2,1)} collective-permute-done((bf16[960,1024]{1,0:T(8,128)(2,1)S(1)}, bf16[960,1024]{1,0:T(8,128)(2,1)}, u32[]{:S(2)}, u32[]{:S(2)}) %collective-permute-start.19) | collective-permute-done | bytes 1966112 | tf_op jit(solution)/shard_map/ppermute | solution.py:52
  419.8 38.5 %collective-permute-done.10 = bf16[960,1024]{1,0:T(8,128)(2,1)S(1)} collective-permute-done((bf16[960,1024]{1,0:T(8,128)(2,1)S(1)}, bf16[960,1024]{1,0:T(8,128)(2,1)S(1)}, u32[]{:S(2)}, u32[]{:S(2)}) %collective-permute-start.10) | collective-permute-done | bytes 1966112 | tf_op jit(solution)/shard_map/ppermute | solution.py:52
  460.3 39.3 %collective-permute-done.8 = bf16[960,1024]{1,0:T(8,128)(2,1)S(1)} collective-permute-done((bf16[960,1024]{1,0:T(8,128)(2,1)S(1)}, bf16[960,1024]{1,0:T(8,128)(2,1)S(1)}, u32[]{:S(2)}, u32[]{:S(2)}) %collective-permute-start.8) | collective-permute-done | bytes 1966112 | tf_op jit(solution)/shard_map/ppermute | solution.py:52
  499.6 46.2 %collective-permute-done.18 = bf16[960,1024]{1,0:T(8,128)(2,1)S(1)} collective-permute-done((bf16[960,1024]{1,0:T(8,128)(2,1)S(1)}, bf16[960,1024]{1,0:T(8,128)(2,1)S(1)}, u32[]{:S(2)}, u32[]{:S(2)}) %collective-permute-start.18) | collective-permute-done | bytes 1966112 | tf_op jit(solution)/shard_map/ppermute | solution.py:40
  555.5 83.3 %collective-permute-done.24 = bf16[240,4096]{1,0:T(8,128)(2,1)} collective-permute-done((bf16[240,4096]{1,0:T(8,128)(2,1)}, bf16[240,4096]{1,0:T(8,128)(2,1)}, u32[]{:S(2)}, u32[]{:S(2)}) %collective-permute-start.24) | collective-permute-done | bytes 1966112 | tf_op jit(solution)/shard_map/ppermute | solution.py:40
  639.7 10.1 %scatter_custom_fusion = s32[1920]{0:T(1024)S(1)} fusion(s32[1920]{0:T(1024)S(1)} %get-tuple-element.54, s32[1920]{0:T(1024)S(1)} %get-tuple-element.55, s32[]{:T(128)} %constant.250.clone.1), kind=kCustom, calls=%fused_computation.203 | custom fusion | bytes 7684 | tf_op jit(solution)/shard_map/scatter | solution.py:164
  658.4 25.3 %collective-permute-done.26 = bf16[240,4096]{1,0:T(8,128)(2,1)} collective-permute-done((bf16[240,4096]{1,0:T(8,128)(2,1)}, bf16[240,4096]{1,0:T(8,128)(2,1)}, u32[]{:S(2)}, u32[]{:S(2)}) %collective-permute-start.26) | collective-permute-done | bytes 1966112 | tf_op jit(solution)/shard_map/ppermute | solution.py:40
  692.6 34.6 %collective-permute-done.25 = bf16[240,4096]{1,0:T(8,128)(2,1)S(1)} collective-permute-done((bf16[240,4096]{1,0:T(8,128)(2,1)}, bf16[240,4096]{1,0:T(8,128)(2,1)S(1)}, u32[]{:S(2)}, u32[]{:S(2)}) %collective-permute-start.25) | collective-permute-done | bytes 1966112 | tf_op jit(solution)/shard_map/ppermute | solution.py:48
  731.1 37.2 %collective-permute-done.27 = bf16[240,4096]{1,0:T(8,128)(2,1)S(1)} collective-permute-done((bf16[240,4096]{1,0:T(8,128)(2,1)}, bf16[240,4096]{1,0:T(8,128)(2,1)S(1)}, u32[]{:S(2)}, u32[]{:S(2)}) %collective-permute-start.27) | collective-permute-done | bytes 1966112 | tf_op jit(solution)/shard_map/ppermute | solution.py:48
  769.5 6.8 gather_fusion
  783.2 11.7 %collective-permute-done.29 = bf16[480,512]{1,0:T(8,128)(2,1)S(1)} collective-permute-done((bf16[480,512]{1,0:T(8,128)(2,1)S(1)}, bf16[480,512]{1,0:T(8,128)(2,1)S(1)}, u32[]{:S(2)}, u32[]{:S(2)}) %collective-permute-start.29) | collective-permute-done | bytes 491552 | tf_op jit(solution)/shard_map/ppermute | solution.py:52
  803.4 10.3 %all-to-all-done = bf16[8,60,512]{2,1,0:T(8,128)(2,1)S(1)} async-done(((bf16[8,60,512]{2,1,0:T(8,128)(2,1)}), bf16[8,60,512]{2,1,0:T(8,128)(2,1)S(1)}, u32[]{:S(2)}, u32[]{:S(2)}) %all-to-all-start) | async-done | bytes 491552 | tf_op jit(solution)/shard_map/all_to_all | solution.py:181
  (169 shorter events, 190.3 us)
Async XLA Ops:
  11.7 199.1 %collective-permute-start = (bf16[4096,768]{1,0:T(8,128)(2,1)}, bf16[4096,768]{1,0:T(8,128)(2,1)}, u32[]{:S(2)}, u32[]{:S(2)}) collective-permute-start(bf16[4096,768]{1,0:T(8,128)(2,1)} %pad_maximum_fusion), channel_id=1, source_target_pairs={{0,4},{4,0},{8,12},{12,8},{16,20},{20,16},{24,28},{28,24},{1,5},{5... | collective-permute-start | bytes 18874376 | tf_op jit(solution)/shard_map/ppermute | solution.py:48
  33.9 86.4 %collective-permute-start.4 = (bf16[960,1024]{1,0:T(8,128)(2,1)S(1)}, bf16[960,1024]{1,0:T(8,128)(2,1)}, u32[]{:S(2)}, u32[]{:S(2)}) collective-permute-start(bf16[960,1024]{1,0:T(8,128)(2,1)S(1)} %get-tuple-element.33), channel_id=1, source_target_pairs={{0,8},{4,12},{8,0},{12,4},{16,24},{20,28},{24,16},{28,20},{1,9},{5... | collective-permute-start | bytes 5898248 | tf_op jit(solution)/shard_map/ppermute | solution.py:40
  35.4 87.2 %collective-permute-start.1 = (bf16[960,1024]{1,0:T(8,128)(2,1)S(1)}, bf16[960,1024]{1,0:T(8,128)(2,1)}, u32[]{:S(2)}, u32[]{:S(2)}) collective-permute-start(bf16[960,1024]{1,0:T(8,128)(2,1)S(1)} %get-tuple-element.33), channel_id=1, source_target_pairs={{0,16},{4,20},{8,24},{12,28},{16,0},{20,4},{24,8},{28,12},{1,17},{... | collective-permute-start | bytes 5898248 | tf_op jit(solution)/shard_map/ppermute | solution.py:40
  120.3 46.1 %collective-permute-start.5 = (bf16[960,1024]{1,0:T(8,128)(2,1)}, bf16[960,1024]{1,0:T(8,128)(2,1)}, u32[]{:S(2)}, u32[]{:S(2)}) collective-permute-start(bf16[960,1024]{1,0:T(8,128)(2,1)} %collective-permute-done.4), channel_id=1, source_target_pairs={{0,2},{1,3},{2,0},{3,1},{4,6},{5,7},{6,4},{7,5},{8,10},{9,11},{10,... | collective-permute-start | bytes 5898248 | tf_op jit(solution)/shard_map/ppermute | solution.py:52
  122.6 83.5 %collective-permute-start.2 = (bf16[960,1024]{1,0:T(8,128)(2,1)}, bf16[960,1024]{1,0:T(8,128)(2,1)}, u32[]{:S(2)}, u32[]{:S(2)}) collective-permute-start(bf16[960,1024]{1,0:T(8,128)(2,1)} %collective-permute-done.1), channel_id=1, source_target_pairs={{0,2},{1,3},{2,0},{3,1},{4,6},{5,7},{6,4},{7,5},{8,10},{9,11},{10,... | collective-permute-start | bytes 5898248 | tf_op jit(solution)/shard_map/ppermute | solution.py:52
  124.1 85.0 %collective-permute-start.11 = (bf16[960,1024]{1,0:T(8,128)(2,1)}, bf16[960,1024]{1,0:T(8,128)(2,1)S(1)}, u32[]{:S(2)}, u32[]{:S(2)}) collective-permute-start(bf16[960,1024]{1,0:T(8,128)(2,1)} %collective-permute-done.1), channel_id=1, source_target_pairs={{0,8},{4,12},{8,0},{12,4},{16,24},{20,28},{24,16},{28,20},{1,9},{5... | collective-permute-start | bytes 5898248 | tf_op jit(solution)/shard_map/ppermute | solution.py:40
  169.4 85.3 %collective-permute-start.6 = (bf16[960,2048]{1,0:T(8,128)(2,1)}, bf16[960,2048]{1,0:T(8,128)(2,1)}, u32[]{:S(2)}, u32[]{:S(2)}) collective-permute-start(bf16[960,2048]{1,0:T(8,128)(2,1)} %constant_dynamic-update-slice_fusion.2), channel_id=1, source_target_pairs={{0,1},{1,0},{2,3},{3,2},{4,5},{5,4},{6,7},{7,6},{8,9},{9,8},{10,11... | collective-permute-start | bytes 11796488 | tf_op jit(solution)/shard_map/ppermute | solution.py:55
  209.1 67.9 %collective-permute-start.3 = (bf16[960,2048]{1,0:T(8,128)(2,1)}, bf16[960,2048]{1,0:T(8,128)(2,1)}, u32[]{:S(2)}, u32[]{:S(2)}) collective-permute-start(bf16[960,2048]{1,0:T(8,128)(2,1)} %constant_dynamic-update-slice_fusion), channel_id=1, source_target_pairs={{0,1},{1,0},{2,3},{3,2},{4,5},{5,4},{6,7},{7,6},{8,9},{9,8},{10,11... | collective-permute-start | bytes 11796488 | tf_op jit(solution)/shard_map/ppermute | solution.py:55
  209.1 45.2 %collective-permute-start.12 = (bf16[960,1024]{1,0:T(8,128)(2,1)S(1)}, bf16[960,1024]{1,0:T(8,128)(2,1)S(1)}, u32[]{:S(2)}, u32[]{:S(2)}) collective-permute-start(bf16[960,1024]{1,0:T(8,128)(2,1)S(1)} %collective-permute-done.11), channel_id=1, source_target_pairs={{0,2},{1,3},{2,0},{3,1},{4,6},{5,7},{6,4},{7,5},{8,10},{9,11},{10,... | collective-permute-start | bytes 5898248 | tf_op jit(solution)/shard_map/ppermute | solution.py:52
  254.6 43.7 %collective-permute-start.13 = (bf16[960,2048]{1,0:T(8,128)(2,1)S(1)}, bf16[960,2048]{1,0:T(8,128)(2,1)}, u32[]{:S(2)}, u32[]{:S(2)}) collective-permute-start(bf16[960,2048]{1,0:T(8,128)(2,1)S(1)} %constant_dynamic-update-slice_fusion.4), channel_id=1, source_target_pairs={{0,1},{1,0},{2,3},{3,2},{4,5},{5,4},{6,7},{7,6},{8,9},{9,8},{10,11... | collective-permute-start | bytes 11796488 | tf_op jit(solution)/shard_map/ppermute | solution.py:55
  328.3 45.7 %collective-permute-start.16 = (bf16[960,1024]{1,0:T(8,128)(2,1)S(1)}, bf16[960,1024]{1,0:T(8,128)(2,1)S(1)}, u32[]{:S(2)}, u32[]{:S(2)}) collective-permute-start(bf16[960,1024]{1,0:T(8,128)(2,1)S(1)} %slice.118), channel_id=1, source_target_pairs={{0,2},{1,3},{2,0},{3,1},{4,6},{5,7},{6,4},{7,5},{8,10},{9,11},{10,... | collective-permute-start | bytes 5898248 | tf_op jit(solution)/shard_map/ppermute | solution.py:52
  332.5 83.8 %collective-permute-start.19 = (bf16[960,1024]{1,0:T(8,128)(2,1)S(1)}, bf16[960,1024]{1,0:T(8,128)(2,1)}, u32[]{:S(2)}, u32[]{:S(2)}) collective-permute-start(bf16[960,1024]{1,0:T(8,128)(2,1)S(1)} %slice.117), channel_id=1, source_target_pairs={{0,2},{1,3},{2,0},{3,1},{4,6},{5,7},{6,4},{7,5},{8,10},{9,11},{10,... | collective-permute-start | bytes 5898248 | tf_op jit(solution)/shard_map/ppermute | solution.py:52
  338.0 120.3 %collective-permute-start.10 = (bf16[960,1024]{1,0:T(8,128)(2,1)S(1)}, bf16[960,1024]{1,0:T(8,128)(2,1)S(1)}, u32[]{:S(2)}, u32[]{:S(2)}) collective-permute-start(bf16[960,1024]{1,0:T(8,128)(2,1)S(1)} %slice.119), channel_id=1, source_target_pairs={{0,2},{1,3},{2,0},{3,1},{4,6},{5,7},{6,4},{7,5},{8,10},{9,11},{10,... | collective-permute-start | bytes 5898248 | tf_op jit(solution)/shard_map/ppermute | solution.py:52
  376.5 81.8 %collective-permute-start.17 = (bf16[960,1024]{1,0:T(8,128)(2,1)}, bf16[960,1024]{1,0:T(8,128)(2,1)S(1)}, u32[]{:S(2)}, u32[]{:S(2)}) collective-permute-start(bf16[960,1024]{1,0:T(8,128)(2,1)} %fusion.7), channel_id=1, source_target_pairs={{0,8},{4,12},{8,0},{12,4},{16,24},{20,28},{24,16},{28,20},{1,9},{5... | collective-permute-start | bytes 5898248 | tf_op jit(solution)/shard_map/ppermute | solution.py:40
  381.5 118.1 %collective-permute-start.8 = (bf16[960,1024]{1,0:T(8,128)(2,1)S(1)}, bf16[960,1024]{1,0:T(8,128)(2,1)S(1)}, u32[]{:S(2)}, u32[]{:S(2)}) collective-permute-start(bf16[960,1024]{1,0:T(8,128)(2,1)S(1)} %slice.120), channel_id=1, source_target_pairs={{0,2},{1,3},{2,0},{3,1},{4,6},{5,7},{6,4},{7,5},{8,10},{9,11},{10,... | collective-permute-start | bytes 5898248 | tf_op jit(solution)/shard_map/ppermute | solution.py:52
  419.8 79.8 %collective-permute-start.20 = (bf16[960,1024]{1,0:T(8,128)(2,1)}, bf16[960,1024]{1,0:T(8,128)(2,1)S(1)}, u32[]{:S(2)}, u32[]{:S(2)}) collective-permute-start(bf16[960,1024]{1,0:T(8,128)(2,1)} %fusion.6), channel_id=1, source_target_pairs={{0,8},{4,12},{8,0},{12,4},{16,24},{20,28},{24,16},{28,20},{1,9},{5... | collective-permute-start | bytes 5898248 | tf_op jit(solution)/shard_map/ppermute | solution.py:40
  459.5 86.3 %collective-permute-start.18 = (bf16[960,1024]{1,0:T(8,128)(2,1)S(1)}, bf16[960,1024]{1,0:T(8,128)(2,1)S(1)}, u32[]{:S(2)}, u32[]{:S(2)}) collective-permute-start(bf16[960,1024]{1,0:T(8,128)(2,1)S(1)} %fusion.9), channel_id=1, source_target_pairs={{0,16},{4,20},{8,24},{12,28},{16,0},{20,4},{24,8},{28,12},{1,17},{... | collective-permute-start | bytes 5898248 | tf_op jit(solution)/shard_map/ppermute | solution.py:40
  552.2 86.6 %collective-permute-start.24 = (bf16[240,4096]{1,0:T(8,128)(2,1)}, bf16[240,4096]{1,0:T(8,128)(2,1)}, u32[]{:S(2)}, u32[]{:S(2)}) collective-permute-start(bf16[240,4096]{1,0:T(8,128)(2,1)} %reshape.73), channel_id=1, source_target_pairs={{0,16},{4,20},{8,24},{12,28},{16,0},{20,4},{24,8},{28,12},{1,17},{... | collective-permute-start | bytes 5898248 | tf_op jit(solution)/shard_map/ppermute | solution.py:40
  552.2 86.9 %collective-permute-start.22 = (bf16[240,4096]{1,0:T(8,128)(2,1)}, bf16[240,4096]{1,0:T(8,128)(2,1)}, u32[]{:S(2)}, u32[]{:S(2)}) collective-permute-start(bf16[240,4096]{1,0:T(8,128)(2,1)} %reshape.73), channel_id=1, source_target_pairs={{0,8},{4,12},{8,0},{12,4},{16,24},{20,28},{24,16},{28,20},{1,9},{5... | collective-permute-start | bytes 5898248 | tf_op jit(solution)/shard_map/ppermute | solution.py:40
  554.9 100.7 %collective-permute-start.21 = (bf16[240,4096]{1,0:T(8,128)(2,1)}, bf16[240,4096]{1,0:T(8,128)(2,1)}, u32[]{:S(2)}, u32[]{:S(2)}) collective-permute-start(bf16[240,4096]{1,0:T(8,128)(2,1)} %reshape.73), channel_id=1, source_target_pairs={{0,4},{4,0},{8,12},{12,8},{16,20},{20,16},{24,28},{28,24},{1,5},{5... | collective-permute-start | bytes 5898248 | tf_op jit(solution)/shard_map/ppermute | solution.py:48
  638.7 45.0 %collective-permute-start.26 = (bf16[240,4096]{1,0:T(8,128)(2,1)}, bf16[240,4096]{1,0:T(8,128)(2,1)}, u32[]{:S(2)}, u32[]{:S(2)}) collective-permute-start(bf16[240,4096]{1,0:T(8,128)(2,1)} %collective-permute-done.24), channel_id=1, source_target_pairs={{0,8},{4,12},{8,0},{12,4},{16,24},{20,28},{24,16},{28,20},{1,9},{5... | collective-permute-start | bytes 5898248 | tf_op jit(solution)/shard_map/ppermute | solution.py:40
  639.1 48.0 %collective-permute-start.23 = (bf16[240,4096]{1,0:T(8,128)(2,1)}, bf16[240,4096]{1,0:T(8,128)(2,1)}, u32[]{:S(2)}, u32[]{:S(2)}) collective-permute-start(bf16[240,4096]{1,0:T(8,128)(2,1)} %collective-permute-done.22), channel_id=1, source_target_pairs={{0,4},{4,0},{8,12},{12,8},{16,20},{20,16},{24,28},{28,24},{1,5},{5... | collective-permute-start | bytes 5898248 | tf_op jit(solution)/shard_map/ppermute | solution.py:48
  649.9 77.3 %collective-permute-start.25 = (bf16[240,4096]{1,0:T(8,128)(2,1)}, bf16[240,4096]{1,0:T(8,128)(2,1)S(1)}, u32[]{:S(2)}, u32[]{:S(2)}) collective-permute-start(bf16[240,4096]{1,0:T(8,128)(2,1)} %collective-permute-done.24), channel_id=1, source_target_pairs={{0,4},{4,0},{8,12},{12,8},{16,20},{20,16},{24,28},{28,24},{1,5},{5... | collective-permute-start | bytes 5898248 | tf_op jit(solution)/shard_map/ppermute | solution.py:48
  683.7 84.6 %collective-permute-start.27 = (bf16[240,4096]{1,0:T(8,128)(2,1)}, bf16[240,4096]{1,0:T(8,128)(2,1)S(1)}, u32[]{:S(2)}, u32[]{:S(2)}) collective-permute-start(bf16[240,4096]{1,0:T(8,128)(2,1)} %collective-permute-done.26), channel_id=1, source_target_pairs={{0,4},{4,0},{8,12},{12,8},{16,20},{20,16},{24,28},{28,24},{1,5},{5... | collective-permute-start | bytes 5898248 | tf_op jit(solution)/shard_map/ppermute | solution.py:48
  (30 other events, 659.4 us)

commit v3 on v2

--- a/solution.py
+++ b/solution.py
@@ -78,13 +78,14 @@
     own_quarter = lax.dynamic_slice_in_dim(normed, mlp_index * feat_width, feat_width, axis=1)
 
     quarters = {1: swap_far(own_quarter, 1), 2: swap_far(own_quarter, 2)}
-    quarters[1], text_rows = lax.optimization_barrier((quarters[1], text_rows))
+    def moved(first):
+        return [first] + [shift_pair(first, t) for t in range(1, pair_count)]
+
+    columns = {1: moved(quarters[1])}
+    columns[1], quarters[2] = lax.optimization_barrier((columns[1], quarters[2]))
     quarters[3] = swap_far(quarters[2], 1)
-    halves = {0: (relative(normed, 1, -1, kept), relative(normed, 1, -1, sent))}
-    for k in (1, 2, 3):
-        first = quarters[k]
-        column = jnp.concatenate([first] + [shift_pair(first, t) for t in range(1, pair_count)], axis=1)
-        halves[k] = (column, swap_core(column))
+    columns[2] = moved(quarters[2])
+    columns[3] = moved(quarters[3])
 
     def with_near(index):
         cut = slice(index * units, (index + 1) * units)
@@ -102,21 +103,28 @@
     def dot_t(a, w):
         return lax.dot_general(a, w, (((1,), (1,)), ((), ())), preferred_element_type=jnp.float32)
 
-    hiddens, from_core, after = {}, {}, None
+    hiddens, from_core, afters = {}, {}, {}
     for k in (0, 1, 2, 3):
-        here, there = halves[k]
-        if after is not None:
-            here, there, _ = lax.optimization_barrier((here, there, after))
+        if k == 0:
+            here, there = relative(normed, 1, -1, kept), relative(normed, 1, -1, sent)
+        else:
+            if k >= 2:
+                columns[k], afters[k - 2] = lax.optimization_barrier((columns[k], afters[k - 2]))
+            here = jnp.concatenate(columns[k], axis=1)
+            there = swap_core(here)
+            here, there, afters[k - 1] = lax.optimization_barrier((here, there, afters[k - 1]))
         if k >= 2:
             here, there, from_core[k - 2] = lax.optimization_barrier((here, there, from_core[k - 2]))
         gate_act = dot(here, gate_rel[0]) + dot(there, gate_rel[1])
         up_act = dot(here, up_rel[0]) + dot(there, up_rel[1])
         hiddens[k] = (jax.nn.silu(gate_act) * up_act).astype(jnp.bfloat16)
-        after = dot_t(hiddens[k], down_sent).astype(jnp.bfloat16)
-        from_core[k] = swap_core(after)
-
-    def over_mlp(k):
-        of_core = dot_t(hiddens[k], down_kept) + from_core[k].astype(jnp.float32)
+        afters[k] = dot_t(hiddens[k], down_sent).astype(jnp.bfloat16)
+        from_core[k] = swap_core(afters[k])
+
+    def over_core(k):
+        return dot_t(hiddens[k], down_kept) + from_core[k].astype(jnp.float32)
+
+    def over_pair(of_core):
         mine = of_core[:, :feat_width]
         for t in range(1, pair_count):
             part = of_core[:, t * feat_width : (t + 1) * feat_width].astype(jnp.bfloat16)
@@ -126,10 +134,17 @@
     def sent_far(x, k):
         return swap_far(x.astype(jnp.bfloat16), k).astype(jnp.float32)
 
-    total = over_mlp(0)
-    farthest = sent_far(over_mlp(3), 1)
-    total = total + sent_far(over_mlp(2) + farthest, 2)
-    total = total + sent_far(over_mlp(1), 1)
+    total = over_pair(over_core(0))
+    total, from_core[3] = lax.optimization_barrier((total, from_core[3]))
+    third = over_core(3)
+    third, from_core[2] = lax.optimization_barrier((third, from_core[2]))
+    second = over_core(2)
+    third = over_pair(third).astype(jnp.bfloat16)
+    third, from_core[1] = lax.optimization_barrier((third, from_core[1]))
+    farthest = sent_far(third, 1)
+    first = over_core(1)
+    total = total + sent_far(over_pair(second) + farthest, 2)
+    total = total + sent_far(over_pair(first), 1)
 
     scale_here = lax.dynamic_slice_in_dim(layer_scale, mlp_index * feat_width, feat_width)
     own_inputs = lax.dynamic_slice_in_dim(patches, mlp_index * feat_width, feat_width, axis=1).astype(jnp.float32)
@@ -164,11 +179,15 @@
         jnp.zeros((bucket_count * capacity,), jnp.int32).at[rows_at].set(slot_place, mode="drop")
     )
 
-    firsts = {0: merged, 1: swap_far(merged, 1), 2: swap_far(merged, 2)}
+    def along_near(first):
+        return [first] + [shift_near(first, t) for t in range(1, near_count)]
+
+    firsts = {1: swap_far(merged, 1), 2: swap_far(merged, 2)}
+    groups = {0: along_near(merged), 1: along_near(firsts[1])}
+    groups[1], firsts[2] = lax.optimization_barrier((groups[1], firsts[2]))
     firsts[3] = swap_far(firsts[2], 1)
-    gathered = []
-    for k in range(far_count):
-        gathered += [firsts[k]] + [shift_near(firsts[k], t) for t in range(1, near_count)]
+    groups[2], groups[3] = along_near(firsts[2]), along_near(firsts[3])
+    gathered = groups[0] + groups[1] + groups[2] + groups[3]
     products = jnp.concatenate([dot(g, weight_cols).astype(jnp.bfloat16) for g in gathered], axis=0)
     picked = jnp.take(products, sources, axis=0)
     out_width = picked.shape[1]

time: 831 us -> 907 us (1.091)
  waiting for transfers between devices: 579 us -> 660 us
    ppermute x5, waiting for transfers between devices: 71.8 us -> 135 us  [shift_near(): return lax.ppermute(x, 'req', perm)]
    ppermute x8, waiting for transfers between devices: 245 us -> 262 us  [shift_pair(): return lax.ppermute(x, 'mlp', perm)]
    ppermute x9, waiting for transfers between devices: 238 us -> 251 us  [swap_far(): return lax.ppermute(x, 'req', perm)]
    ppermute x8, waiting for transfers between devices: 13.7 us -> 2.57 us  [swap_core(): return lax.ppermute(x, 'mlp', [(m, m ^ 1) for m in range(mlp_count)])]
    unnamed x49 -> x58, local copies, waits for them, and re-layouts: 12.7 us -> 20.8 us
  transfers between devices with their start and end apart: 31 -> 31, of which waited for: 18 -> 21; matrix products, arithmetic and copies ran while one was open for 18% -> 16% of each run, Pallas kernels for 0% -> 0%
where the time goes in v3:
time: 907 us; the launch traced here: 897 us
  waiting for transfers between devices  660 us (73%)
  matrix products  107 us (12%)
  local copies, waits for them, and re-layouts  59.1 us (7%)
  starting transfers between devices  36.1 us (4%)
  other arithmetic  32.8 us (4%)
    ppermute x8, waiting for transfers between devices, shift_pair(): return lax.ppermute(x, 'mlp', perm)  262 us
    ppermute x9, waiting for transfers between devices, swap_far(): return lax.ppermute(x, 'req', perm)  251 us
    ppermute x5, waiting for transfers between devices, shift_near(): return lax.ppermute(x, 'req', perm)  135 us
    dot_general x24, matrix products, dot(): return jnp.dot(a, w, preferred_element_type=jnp.float32)  81.4 us
    dot_general x8, matrix products, dot_t(): lax.dot_general(a, w, (((1,), (1,)), ((), ())), preferred_element_type=jn...  25.8 us
    unnamed x58, local copies, waits for them, and re-layouts  20.8 us
  transfers between devices with their start and end apart: 31, of which 21 were waited for; matrix products, arithmetic and copies ran while one was open for 16% of the time, Pallas kernels for 0%

profile of v3, /device:TPU:0, one launch (start us, length us, event | category | flops | bytes accessed | tf_op | source)
XLA Modules:
  0.0 897.1 jit_solution(11480149732112592095)
XLA Ops:
  0.7 8.0 copy.28
  22.4 7.8 fusion.5
  38.0 82.1 %collective-permute-done.1 = bf16[960,1024]{1,0:T(8,128)(2,1)S(1)} collective-permute-done((bf16[960,1024]{1,0:T(8,128)(2,1)S(1)}, bf16[960,1024]{1,0:T(8,128)(2,1)S(1)}, u32[]{:S(2)}, u32[]{:S(2)}) %collective-permute-start.1) | collective-permute-done | bytes 1966112 | tf_op jit(solution)/shard_map/ppermute | solution.py:40
  122.6 41.0 %collective-permute-done.2 = bf16[960,1024]{1,0:T(8,128)(2,1)S(1)} collective-permute-done((bf16[960,1024]{1,0:T(8,128)(2,1)S(1)}, bf16[960,1024]{1,0:T(8,128)(2,1)S(1)}, u32[]{:S(2)}, u32[]{:S(2)}) %collective-permute-start.2) | collective-permute-done | bytes 1966112 | tf_op jit(solution)/shard_map/ppermute | solution.py:52
  167.5 39.0 %collective-permute-done.4 = bf16[960,1024]{1,0:T(8,128)(2,1)} collective-permute-done((bf16[960,1024]{1,0:T(8,128)(2,1)}, bf16[960,1024]{1,0:T(8,128)(2,1)}, u32[]{:S(2)}, u32[]{:S(2)}) %collective-permute-start.4) | collective-permute-done | bytes 1966112 | tf_op jit(solution)/shard_map/ppermute | solution.py:52
  241.8 15.9 %collective-permute-done.10 = bf16[960,1024]{1,0:T(8,128)(2,1)S(1)} collective-permute-done((bf16[960,1024]{1,0:T(8,128)(2,1)S(1)}, bf16[960,1024]{1,0:T(8,128)(2,1)S(1)}, u32[]{:S(2)}, u32[]{:S(2)}) %collective-permute-start.10) | collective-permute-done | bytes 1966112 | tf_op jit(solution)/shard_map/ppermute | solution.py:52
  279.1 5.7 fusion.84
  302.3 5.7 fusion.83
  324.3 43.3 %collective-permute-done.8 = bf16[960,1024]{1,0:T(8,128)(2,1)S(1)} collective-permute-done((bf16[960,1024]{1,0:T(8,128)(2,1)S(1)}, bf16[960,1024]{1,0:T(8,128)(2,1)S(1)}, u32[]{:S(2)}, u32[]{:S(2)}) %collective-permute-start.8) | collective-permute-done | bytes 1966112 | tf_op jit(solution)/shard_map/ppermute | solution.py:52
  376.0 40.7 %collective-permute-done.16 = bf16[960,1024]{1,0:T(8,128)(2,1)S(1)} collective-permute-done((bf16[960,1024]{1,0:T(8,128)(2,1)S(1)}, bf16[960,1024]{1,0:T(8,128)(2,1)S(1)}, u32[]{:S(2)}, u32[]{:S(2)}) %collective-permute-start.16) | collective-permute-done | bytes 1966112 | tf_op jit(solution)/shard_map/ppermute | solution.py:52
  425.1 33.7 %collective-permute-done.15 = bf16[960,1024]{1,0:T(8,128)(2,1)S(1)} collective-permute-done((bf16[960,1024]{1,0:T(8,128)(2,1)S(1)}, bf16[960,1024]{1,0:T(8,128)(2,1)S(1)}, u32[]{:S(2)}, u32[]{:S(2)}) %collective-permute-start.15) | collective-permute-done | bytes 1966112 | tf_op jit(solution)/shard_map/ppermute | solution.py:52
  463.8 35.4 %collective-permute-done.19 = bf16[960,1024]{1,0:T(8,128)(2,1)S(1)} collective-permute-done((bf16[960,1024]{1,0:T(8,128)(2,1)S(1)}, bf16[960,1024]{1,0:T(8,128)(2,1)S(1)}, u32[]{:S(2)}, u32[]{:S(2)}) %collective-permute-start.19) | collective-permute-done | bytes 1966112 | tf_op jit(solution)/shard_map/ppermute | solution.py:52
  500.0 45.0 %collective-permute-done.18 = bf16[960,1024]{1,0:T(8,128)(2,1)S(1)} collective-permute-done((bf16[960,1024]{1,0:T(8,128)(2,1)S(1)}, bf16[960,1024]{1,0:T(8,128)(2,1)S(1)}, u32[]{:S(2)}, u32[]{:S(2)}) %collective-permute-start.18) | collective-permute-done | bytes 1966112 | tf_op jit(solution)/shard_map/ppermute | solution.py:40
  545.0 39.2 %collective-permute-done.20 = bf16[960,1024]{1,0:T(8,128)(2,1)S(1)} collective-permute-done((bf16[960,1024]{1,0:T(8,128)(2,1)S(1)}, bf16[960,1024]{1,0:T(8,128)(2,1)S(1)}, u32[]{:S(2)}, u32[]{:S(2)}) %collective-permute-start.20) | collective-permute-done | bytes 1966112 | tf_op jit(solution)/shard_map/ppermute | solution.py:40
  594.2 80.8 %collective-permute-done.22 = bf16[240,4096]{1,0:T(8,128)(2,1)S(1)} collective-permute-done((bf16[240,4096]{1,0:T(8,128)(2,1)}, bf16[240,4096]{1,0:T(8,128)(2,1)S(1)}, u32[]{:S(2)}, u32[]{:S(2)}) %collective-permute-start.22) | collective-permute-done | bytes 1966112 | tf_op jit(solution)/shard_map/ppermute | solution.py:40
  678.1 42.6 %collective-permute-done.23 = bf16[240,4096]{1,0:T(8,128)(2,1)S(1)} collective-permute-done((bf16[240,4096]{1,0:T(8,128)(2,1)S(1)}, bf16[240,4096]{1,0:T(8,128)(2,1)S(1)}, u32[]{:S(2)}, u32[]{:S(2)}) %collective-permute-start.23) | collective-permute-done | bytes 1966112 | tf_op jit(solution)/shard_map/ppermute | solution.py:48
  722.4 10.1 %scatter_custom_fusion = s32[1920]{0:T(1024)S(1)} fusion(s32[1920]{0:T(1024)S(1)} %get-tuple-element.82, s32[1920]{0:T(1024)S(1)} %get-tuple-element.83, s32[]{:T(128)} %constant.250.clone.1), kind=kCustom, calls=%fused_computation.198 | custom fusion | bytes 7684 | tf_op jit(solution)/shard_map/scatter | solution.py:179
  738.5 24.4 %collective-permute-done.21 = bf16[240,4096]{1,0:T(8,128)(2,1)} collective-permute-done((bf16[240,4096]{1,0:T(8,128)(2,1)}, bf16[240,4096]{1,0:T(8,128)(2,1)}, u32[]{:S(2)}, u32[]{:S(2)}) %collective-permute-start.21) | collective-permute-done | bytes 1966112 | tf_op jit(solution)/shard_map/ppermute | solution.py:48
  772.7 32.3 %collective-permute-done.25 = bf16[240,4096]{1,0:T(8,128)(2,1)S(1)} collective-permute-done((bf16[240,4096]{1,0:T(8,128)(2,1)}, bf16[240,4096]{1,0:T(8,128)(2,1)S(1)}, u32[]{:S(2)}, u32[]{:S(2)}) %collective-permute-start.25) | collective-permute-done | bytes 1966112 | tf_op jit(solution)/shard_map/ppermute | solution.py:48
  808.9 35.3 %collective-permute-done.27 = bf16[240,4096]{1,0:T(8,128)(2,1)S(1)} collective-permute-done((bf16[240,4096]{1,0:T(8,128)(2,1)}, bf16[240,4096]{1,0:T(8,128)(2,1)S(1)}, u32[]{:S(2)}, u32[]{:S(2)}) %collective-permute-start.27) | collective-permute-done | bytes 1966112 | tf_op jit(solution)/shard_map/ppermute | solution.py:48
  845.4 6.8 gather_fusion
  858.2 12.6 %collective-permute-done.29 = bf16[480,512]{1,0:T(8,128)(2,1)S(1)} collective-permute-done((bf16[480,512]{1,0:T(8,128)(2,1)S(1)}, bf16[480,512]{1,0:T(8,128)(2,1)S(1)}, u32[]{:S(2)}, u32[]{:S(2)}) %collective-permute-start.29) | collective-permute-done | bytes 491552 | tf_op jit(solution)/shard_map/ppermute | solution.py:52
  871.9 4.9 all-to-all-start
  880.5 10.3 %all-to-all-done = bf16[8,60,512]{2,1,0:T(8,128)(2,1)S(1)} async-done(((bf16[8,60,512]{2,1,0:T(8,128)(2,1)}), bf16[8,60,512]{2,1,0:T(8,128)(2,1)S(1)}, u32[]{:S(2)}, u32[]{:S(2)}) %all-to-all-start) | async-done | bytes 491552 | tf_op jit(solution)/shard_map/all_to_all | solution.py:200
  (178 shorter events, 192.2 us)
Async XLA Ops:
  11.7 202.4 %collective-permute-start = (bf16[4096,768]{1,0:T(8,128)(2,1)}, bf16[4096,768]{1,0:T(8,128)(2,1)}, u32[]{:S(2)}, u32[]{:S(2)}) collective-permute-start(bf16[4096,768]{1,0:T(8,128)(2,1)} %pad_maximum_fusion), channel_id=1, source_target_pairs={{0,4},{4,0},{8,12},{12,8},{16,20},{20,16},{24,28},{28,24},{1,5},{5... | collective-permute-start | bytes 18874376 | tf_op jit(solution)/shard_map/ppermute | solution.py:48
  33.9 86.3 %collective-permute-start.1 = (bf16[960,1024]{1,0:T(8,128)(2,1)S(1)}, bf16[960,1024]{1,0:T(8,128)(2,1)S(1)}, u32[]{:S(2)}, u32[]{:S(2)}) collective-permute-start(bf16[960,1024]{1,0:T(8,128)(2,1)S(1)} %get-tuple-element.61), channel_id=1, source_target_pairs={{0,8},{4,12},{8,0},{12,4},{16,24},{20,28},{24,16},{28,20},{1,9},{5... | collective-permute-start | bytes 5898248 | tf_op jit(solution)/shard_map/ppermute | solution.py:40
  35.4 87.2 %collective-permute-start.3 = (bf16[960,1024]{1,0:T(8,128)(2,1)S(1)}, bf16[960,1024]{1,0:T(8,128)(2,1)}, u32[]{:S(2)}, u32[]{:S(2)}) collective-permute-start(bf16[960,1024]{1,0:T(8,128)(2,1)S(1)} %get-tuple-element.61), channel_id=1, source_target_pairs={{0,16},{4,20},{8,24},{12,28},{16,0},{20,4},{24,8},{28,12},{1,17},{... | collective-permute-start | bytes 5898248 | tf_op jit(solution)/shard_map/ppermute | solution.py:40
  120.2 43.5 %collective-permute-start.2 = (bf16[960,1024]{1,0:T(8,128)(2,1)S(1)}, bf16[960,1024]{1,0:T(8,128)(2,1)S(1)}, u32[]{:S(2)}, u32[]{:S(2)}) collective-permute-start(bf16[960,1024]{1,0:T(8,128)(2,1)S(1)} %collective-permute-done.1), channel_id=1, source_target_pairs={{0,2},{1,3},{2,0},{3,1},{4,6},{5,7},{6,4},{7,5},{8,10},{9,11},{10,... | collective-permute-start | bytes 5898248 | tf_op jit(solution)/shard_map/ppermute | solution.py:52
  165.2 47.4 %collective-permute-start.9 = (bf16[960,1024]{1,0:T(8,128)(2,1)}, bf16[960,1024]{1,0:T(8,128)(2,1)S(1)}, u32[]{:S(2)}, u32[]{:S(2)}) collective-permute-start(bf16[960,1024]{1,0:T(8,128)(2,1)} %collective-permute-done.3), channel_id=1, source_target_pairs={{0,8},{4,12},{8,0},{12,4},{16,24},{20,28},{24,16},{28,20},{1,9},{5... | collective-permute-start | bytes 5898248 | tf_op jit(solution)/shard_map/ppermute | solution.py:40
  167.5 90.7 %collective-permute-start.6 = (bf16[960,2048]{1,0:T(8,128)(2,1)S(1)}, bf16[960,2048]{1,0:T(8,128)(2,1)}, u32[]{:S(2)}, u32[]{:S(2)}) collective-permute-start(bf16[960,2048]{1,0:T(8,128)(2,1)S(1)} %constant_dynamic-update-slice_fusion.2), channel_id=1, source_target_pairs={{0,1},{1,0},{2,3},{3,2},{4,5},{5,4},{6,7},{7,6},{8,9},{9,8},{10,11... | collective-permute-start | bytes 11796488 | tf_op jit(solution)/shard_map/ppermute | solution.py:55
  212.6 66.6 %collective-permute-start.5 = (bf16[960,2048]{1,0:T(8,128)(2,1)}, bf16[960,2048]{1,0:T(8,128)(2,1)}, u32[]{:S(2)}, u32[]{:S(2)}) collective-permute-start(bf16[960,2048]{1,0:T(8,128)(2,1)} %constant_dynamic-update-slice_fusion), channel_id=1, source_target_pairs={{0,1},{1,0},{2,3},{3,2},{4,5},{5,4},{6,7},{7,6},{8,9},{9,8},{10,11... | collective-permute-start | bytes 11796488 | tf_op jit(solution)/shard_map/ppermute | solution.py:55
  212.6 45.2 %collective-permute-start.10 = (bf16[960,1024]{1,0:T(8,128)(2,1)S(1)}, bf16[960,1024]{1,0:T(8,128)(2,1)S(1)}, u32[]{:S(2)}, u32[]{:S(2)}) collective-permute-start(bf16[960,1024]{1,0:T(8,128)(2,1)S(1)} %collective-permute-done.9), channel_id=1, source_target_pairs={{0,2},{1,3},{2,0},{3,1},{4,6},{5,7},{6,4},{7,5},{8,10},{9,11},{10,... | collective-permute-start | bytes 5898248 | tf_op jit(solution)/shard_map/ppermute | solution.py:52
  258.2 44.1 %collective-permute-start.11 = (bf16[960,2048]{1,0:T(8,128)(2,1)S(1)}, bf16[960,2048]{1,0:T(8,128)(2,1)}, u32[]{:S(2)}, u32[]{:S(2)}) collective-permute-start(bf16[960,2048]{1,0:T(8,128)(2,1)S(1)} %constant_dynamic-update-slice_fusion.4), channel_id=1, source_target_pairs={{0,1},{1,0},{2,3},{3,2},{4,5},{5,4},{6,7},{7,6},{8,9},{9,8},{10,11... | collective-permute-start | bytes 11796488 | tf_op jit(solution)/shard_map/ppermute | solution.py:55
  319.5 48.7 %collective-permute-start.13 = (bf16[960,2048]{1,0:T(8,128)(2,1)S(1)}, bf16[960,2048]{1,0:T(8,128)(2,1)S(1)}, u32[]{:S(2)}, u32[]{:S(2)}) collective-permute-start(bf16[960,2048]{1,0:T(8,128)(2,1)S(1)} %convolution_convert_fusion), channel_id=1, source_target_pairs={{0,1},{1,0},{2,3},{3,2},{4,5},{5,4},{6,7},{7,6},{8,9},{9,8},{10,11... | collective-permute-start | bytes 11796488 | tf_op jit(solution)/shard_map/ppermute | solution.py:55
  319.6 50.9 %collective-permute-start.14 = (bf16[960,2048]{1,0:T(8,128)(2,1)}, bf16[960,2048]{1,0:T(8,128)(2,1)S(1)}, u32[]{:S(2)}, u32[]{:S(2)}) collective-permute-start(bf16[960,2048]{1,0:T(8,128)(2,1)} %convolution_convert_fusion.1), channel_id=1, source_target_pairs={{0,1},{1,0},{2,3},{3,2},{4,5},{5,4},{6,7},{7,6},{8,9},{9,8},{10,11... | collective-permute-start | bytes 11796488 | tf_op jit(solution)/shard_map/ppermute | solution.py:55
  322.7 44.9 %collective-permute-start.8 = (bf16[960,1024]{1,0:T(8,128)(2,1)S(1)}, bf16[960,1024]{1,0:T(8,128)(2,1)S(1)}, u32[]{:S(2)}, u32[]{:S(2)}) collective-permute-start(bf16[960,1024]{1,0:T(8,128)(2,1)S(1)} %slice.107), channel_id=1, source_target_pairs={{0,2},{1,3},{2,0},{3,1},{4,6},{5,7},{6,4},{7,5},{8,10},{9,11},{10,... | collective-permute-start | bytes 5898248 | tf_op jit(solution)/shard_map/ppermute | solution.py:52
  370.9 45.8 %collective-permute-start.16 = (bf16[960,1024]{1,0:T(8,128)(2,1)S(1)}, bf16[960,1024]{1,0:T(8,128)(2,1)S(1)}, u32[]{:S(2)}, u32[]{:S(2)}) collective-permute-start(bf16[960,1024]{1,0:T(8,128)(2,1)S(1)} %slice.105), channel_id=1, source_target_pairs={{0,2},{1,3},{2,0},{3,1},{4,6},{5,7},{6,4},{7,5},{8,10},{9,11},{10,... | collective-permute-start | bytes 5898248 | tf_op jit(solution)/shard_map/ppermute | solution.py:52
  375.4 83.4 %collective-permute-start.15 = (bf16[960,1024]{1,0:T(8,128)(2,1)S(1)}, bf16[960,1024]{1,0:T(8,128)(2,1)S(1)}, u32[]{:S(2)}, u32[]{:S(2)}) collective-permute-start(bf16[960,1024]{1,0:T(8,128)(2,1)S(1)} %slice.106), channel_id=1, source_target_pairs={{0,2},{1,3},{2,0},{3,1},{4,6},{5,7},{6,4},{7,5},{8,10},{9,11},{10,... | collective-permute-start | bytes 5898248 | tf_op jit(solution)/shard_map/ppermute | solution.py:52
  423.5 75.6 %collective-permute-start.19 = (bf16[960,1024]{1,0:T(8,128)(2,1)S(1)}, bf16[960,1024]{1,0:T(8,128)(2,1)S(1)}, u32[]{:S(2)}, u32[]{:S(2)}) collective-permute-start(bf16[960,1024]{1,0:T(8,128)(2,1)S(1)} %slice.104), channel_id=1, source_target_pairs={{0,2},{1,3},{2,0},{3,1},{4,6},{5,7},{6,4},{7,5},{8,10},{9,11},{10,... | collective-permute-start | bytes 5898248 | tf_op jit(solution)/shard_map/ppermute | solution.py:52
  461.5 83.5 %collective-permute-start.18 = (bf16[960,1024]{1,0:T(8,128)(2,1)S(1)}, bf16[960,1024]{1,0:T(8,128)(2,1)S(1)}, u32[]{:S(2)}, u32[]{:S(2)}) collective-permute-start(bf16[960,1024]{1,0:T(8,128)(2,1)S(1)} %fusion.8), channel_id=1, source_target_pairs={{0,16},{4,20},{8,24},{12,28},{16,0},{20,4},{24,8},{28,12},{1,17},{... | collective-permute-start | bytes 5898248 | tf_op jit(solution)/shard_map/ppermute | solution.py:40
  499.9 84.3 %collective-permute-start.20 = (bf16[960,1024]{1,0:T(8,128)(2,1)S(1)}, bf16[960,1024]{1,0:T(8,128)(2,1)S(1)}, u32[]{:S(2)}, u32[]{:S(2)}) collective-permute-start(bf16[960,1024]{1,0:T(8,128)(2,1)S(1)} %fusion.6), channel_id=1, source_target_pairs={{0,8},{4,12},{8,0},{12,4},{16,24},{20,28},{24,16},{28,20},{1,9},{5... | collective-permute-start | bytes 5898248 | tf_op jit(solution)/shard_map/ppermute | solution.py:40
  590.1 84.8 %collective-permute-start.22 = (bf16[240,4096]{1,0:T(8,128)(2,1)}, bf16[240,4096]{1,0:T(8,128)(2,1)S(1)}, u32[]{:S(2)}, u32[]{:S(2)}) collective-permute-start(bf16[240,4096]{1,0:T(8,128)(2,1)} %reshape.73), channel_id=1, source_target_pairs={{0,8},{4,12},{8,0},{12,4},{16,24},{20,28},{24,16},{28,20},{1,9},{5... | collective-permute-start | bytes 5898248 | tf_op jit(solution)/shard_map/ppermute | solution.py:40
  590.1 88.0 %collective-permute-start.24 = (bf16[240,4096]{1,0:T(8,128)(2,1)}, bf16[240,4096]{1,0:T(8,128)(2,1)}, u32[]{:S(2)}, u32[]{:S(2)}) collective-permute-start(bf16[240,4096]{1,0:T(8,128)(2,1)} %reshape.73), channel_id=1, source_target_pairs={{0,16},{4,20},{8,24},{12,28},{16,0},{20,4},{24,8},{28,12},{1,17},{... | collective-permute-start | bytes 5898248 | tf_op jit(solution)/shard_map/ppermute | solution.py:40
  674.9 45.8 %collective-permute-start.23 = (bf16[240,4096]{1,0:T(8,128)(2,1)S(1)}, bf16[240,4096]{1,0:T(8,128)(2,1)S(1)}, u32[]{:S(2)}, u32[]{:S(2)}) collective-permute-start(bf16[240,4096]{1,0:T(8,128)(2,1)S(1)} %collective-permute-done.22), channel_id=1, source_target_pairs={{0,4},{4,0},{8,12},{12,8},{16,20},{20,16},{24,28},{28,24},{1,5},{5... | collective-permute-start | bytes 5898248 | tf_op jit(solution)/shard_map/ppermute | solution.py:48
  676.6 86.3 %collective-permute-start.21 = (bf16[240,4096]{1,0:T(8,128)(2,1)}, bf16[240,4096]{1,0:T(8,128)(2,1)}, u32[]{:S(2)}, u32[]{:S(2)}) collective-permute-start(bf16[240,4096]{1,0:T(8,128)(2,1)} %reshape.73), channel_id=1, source_target_pairs={{0,4},{4,0},{8,12},{12,8},{16,20},{20,16},{24,28},{28,24},{1,5},{5... | collective-permute-start | bytes 5898248 | tf_op jit(solution)/shard_map/ppermute | solution.py:48
  722.0 43.7 %collective-permute-start.26 = (bf16[240,4096]{1,0:T(8,128)(2,1)}, bf16[240,4096]{1,0:T(8,128)(2,1)}, u32[]{:S(2)}, u32[]{:S(2)}) collective-permute-start(bf16[240,4096]{1,0:T(8,128)(2,1)} %collective-permute-done.24), channel_id=1, source_target_pairs={{0,8},{4,12},{8,0},{12,4},{16,24},{20,28},{24,16},{28,20},{1,9},{5... | collective-permute-start | bytes 5898248 | tf_op jit(solution)/shard_map/ppermute | solution.py:40
  732.6 72.3 %collective-permute-start.25 = (bf16[240,4096]{1,0:T(8,128)(2,1)}, bf16[240,4096]{1,0:T(8,128)(2,1)S(1)}, u32[]{:S(2)}, u32[]{:S(2)}) collective-permute-start(bf16[240,4096]{1,0:T(8,128)(2,1)} %collective-permute-done.24), channel_id=1, source_target_pairs={{0,4},{4,0},{8,12},{12,8},{16,20},{20,16},{24,28},{28,24},{1,5},{5... | collective-permute-start | bytes 5898248 | tf_op jit(solution)/shard_map/ppermute | solution.py:48
  765.7 78.5 %collective-permute-start.27 = (bf16[240,4096]{1,0:T(8,128)(2,1)}, bf16[240,4096]{1,0:T(8,128)(2,1)S(1)}, u32[]{:S(2)}, u32[]{:S(2)}) collective-permute-start(bf16[240,4096]{1,0:T(8,128)(2,1)} %collective-permute-done.26), channel_id=1, source_target_pairs={{0,4},{4,0},{8,12},{12,8},{16,20},{20,16},{24,28},{28,24},{1,5},{5... | collective-permute-start | bytes 5898248 | tf_op jit(solution)/shard_map/ppermute | solution.py:48
  (34 other events, 805.2 us)
